TPU v7x, 256 devices: a whole 4x4x8 slice. The times are simulated.
256 devices in a mesh: section: 4 (over y), ctx: 8 (over z), exp: 8 (over x, core).
Axes of the slice: x: 4, y: 4, z: 8, core: 2. Of those that a mesh axis runs over, the one named last changes fastest.
Arguments:
- hidden_in: bfloat16 [4, 8, 1024, 4096], P('section', 'exp', 'ctx'), may hold values from -6 to 6
- queries: bfloat16 [4, 8, 1024, 4096], P('section', 'exp', 'ctx'), may hold values from -6 to 6
- keys: bfloat16 [4, 8, 1024, 256], P('section', 'exp', 'ctx'), may hold values from -6 to 6
- values: bfloat16 [4, 8, 1024, 256], P('section', 'exp', 'ctx'), may hold values from -6 to 6
- out_weight: bfloat16 [4, 4096, 4096], P('section', 'ctx'), may hold values from -0.5 to 0.5
- norm_gain: bfloat16 [4, 4096], P('section'), may hold values from 0.5 to 1.5
- w_gate: bfloat16 [4, 8, 4096, 1536], P('section', 'exp', None, 'ctx'), may hold values from -0.09375 to 0.09375
- w_up: bfloat16 [4, 8, 4096, 1536], P('section', 'exp', None, 'ctx'), may hold values from -0.09375 to 0.09375
- w_down_t: bfloat16 [4, 8, 4096, 1536], P('section', 'exp', None, 'ctx'), may hold values from -0.15625 to 0.15625
- expert_ids: int32 [4, 8, 1024, 1], P('section', 'exp', 'ctx'), may hold values from 0 to 7; in each aligned block of 128 rows (0 to 127, 128 to 255, ..., all dimensions but the last counted through in order) at most 20 rows name the same one
- route_gates: float32 [4, 8, 1024, 1], P('section', 'exp', 'ctx'), may hold values from 0.1 to 1
Outputs:
- next_input: bfloat16 [4, 8, 1024, 4096], P('section', 'exp', 'ctx')
Inputs may be any that keep to these rules, and one draw needn't show every extreme that they name: `expert_ids`: within the rows of one device (aligned blocks of 128 positions of a sequence, routes taken together), no expert is named by more than 20 routes.
All inputs are finite; a program needn't handle non-finite values.
Results may differ from a plain program's by a relative error of at most 0.018.
Values may be sent and summed in bfloat16 or wider, within the bound.
A program may use at most 128 MiB of HBM per device.

v0:
```python
import math

import jax
import jax.numpy as jnp
from jax import lax
from jax.sharding import PartitionSpec as P

D = 4096
QUERY_HEADS = 32
KEY_VALUE_HEADS = 2
HEAD_SIZE = 128


def passed_along(array, axis, by):
    count = lax.axis_size(axis)
    return lax.ppermute(array, axis, [(i, (i + by) % count) for i in range(count)])


def expand_rows(rows_here, gate_shard, up_shard):
    gate_part = jnp.dot(rows_here, gate_shard, preferred_element_type=jnp.float32)
    up_part = jnp.dot(rows_here, up_shard, preferred_element_type=jnp.float32)
    return (jax.nn.silu(gate_part) * up_part).astype(jnp.bfloat16)


def shrink_rows(hidden, down_shard):
    return lax.dot_general(
        hidden, down_shard, (((1,), (1,)), ((), ())), preferred_element_type=jnp.float32
    )


def per_device(
    hidden_in,
    queries,
    keys,
    values,
    out_weight,
    norm_gain,
    w_gate,
    w_up,
    w_down_t,
    expert_ids,
    route_gates,
):
    ctx_count = lax.axis_size("ctx")
    exp_count = lax.axis_size("exp")
    rows_in = hidden_in[0, 0]
    tokens_here = rows_in.shape[0]
    heads_here = QUERY_HEADS // ctx_count
    group_length = QUERY_HEADS // KEY_VALUE_HEADS
    query_split = queries[0, 0].reshape(tokens_here, ctx_count, heads_here * HEAD_SIZE)
    query_local = lax.all_to_all(query_split, "ctx", split_axis=1, concat_axis=0, tiled=True)
    key_all, value_all = (
        lax.all_gather(keys[0, 0], "ctx", axis=0, tiled=True),
        lax.all_gather(values[0, 0], "ctx", axis=0, tiled=True),
    )
    kv_head = lax.axis_index("ctx") * heads_here // group_length
    key_local = lax.dynamic_slice_in_dim(key_all, kv_head * HEAD_SIZE, HEAD_SIZE, 1)
    value_local = lax.dynamic_slice_in_dim(value_all, kv_head * HEAD_SIZE, HEAD_SIZE, 1)
    seq_rows = query_local.shape[0]
    block_rows = min(512, seq_rows)
    block_count = seq_rows // block_rows
    query_blocks = query_local.reshape(block_count, block_rows, heads_here, HEAD_SIZE)
    key_positions = jnp.arange(seq_rows, dtype=jnp.int32)

    def attend_block(operands):
        query_block, first_row = operands
        scores = jnp.einsum(
            "qhd,kd->hqk", query_block, key_local, preferred_element_type=jnp.float32
        ) * (1.0 / math.sqrt(HEAD_SIZE))
        causal = (first_row + jnp.arange(block_rows, dtype=jnp.int32))[:, None] >= key_positions[
            None, :
        ]
        scores = jnp.where(causal[None], scores, -1e30)
        shifted = jnp.exp(scores - jnp.max(scores, axis=-1, keepdims=True))
        probs = (shifted / jnp.sum(shifted, axis=-1, keepdims=True)).astype(jnp.bfloat16)
        mixed = jnp.einsum("hqk,kd->qhd", probs, value_local, preferred_element_type=jnp.float32)
        return mixed.astype(jnp.bfloat16).reshape(block_rows, heads_here * HEAD_SIZE)

    block_starts = jnp.arange(block_count, dtype=jnp.int32) * block_rows
    attended = lax.map(attend_block, (query_blocks, block_starts)).reshape(
        seq_rows, heads_here * HEAD_SIZE
    )
    attn_proj = lax.psum_scatter(
        jnp.dot(attended, out_weight[0], preferred_element_type=jnp.float32).astype(jnp.bfloat16),
        "ctx",
        scatter_dimension=0,
        tiled=True,
    ).astype(jnp.float32)
    residual = rows_in.astype(jnp.float32) + attn_proj
    normed = (
        residual
        * lax.rsqrt(jnp.mean(residual * residual, axis=-1, keepdims=True) + 1e-06)
        * norm_gain[0].astype(jnp.float32)
    ).astype(jnp.bfloat16)
    route_top = expert_ids.shape[-1]
    route_ids = expert_ids[0, 0].reshape(tokens_here * route_top)
    capacity = 5 * tokens_here * route_top // (4 * exp_count)
    onehot = (route_ids[:, None] == jnp.arange(exp_count, dtype=jnp.int32)[None, :]).astype(
        jnp.int32
    )
    rank = jnp.sum((jnp.cumsum(onehot, axis=0) - onehot) * onehot, axis=1)
    slot_of_route = route_ids * capacity + rank
    selector = (
        jnp.arange(exp_count * capacity, dtype=jnp.int32)[:, None] == slot_of_route[None, :]
    ).astype(jnp.bfloat16)
    route_rows = jnp.repeat(normed, route_top, axis=0)
    outgoing = jnp.dot(selector, route_rows, preferred_element_type=jnp.float32).astype(
        jnp.bfloat16
    )
    gate_shard = w_gate[0, 0]
    up_shard = w_up[0, 0]
    down_shard = w_down_t[0, 0]
    fanned = jnp.broadcast_to(
        outgoing.reshape(1, exp_count, capacity, D), (ctx_count, exp_count, capacity, D)
    ).reshape(ctx_count * exp_count, capacity, D)
    arrived = lax.all_to_all(fanned, ("ctx", "exp"), split_axis=0, concat_axis=0, tiled=True)
    arrived_rows = arrived.reshape(ctx_count * exp_count * capacity, D)
    shard_out = shrink_rows(expand_rows(arrived_rows, gate_shard, up_shard), down_shard).astype(
        jnp.bfloat16
    )
    returned = lax.all_to_all(
        shard_out.reshape(ctx_count * exp_count, capacity, D),
        ("ctx", "exp"),
        split_axis=0,
        concat_axis=0,
        tiled=True,
    )
    expert_out = jnp.sum(
        returned.reshape(ctx_count, exp_count * capacity, D), axis=0, dtype=jnp.float32
    ).astype(jnp.bfloat16)
    routed = lax.dot_general(
        selector, expert_out, (((0,), (0,)), ((), ())), preferred_element_type=jnp.float32
    )
    mixture = jnp.sum(
        routed.reshape(tokens_here, route_top, D) * route_gates[0, 0][:, :, None], axis=1
    )
    layer_out = (residual + mixture).astype(jnp.bfloat16)
    moved = passed_along(layer_out, "section", 1)
    return moved.reshape(1, 1, tokens_here, D)


def solution(mesh):
    return jax.shard_map(
        per_device,
        mesh=mesh,
        in_specs=(
            P("section", "exp", "ctx", None),
            P("section", "exp", "ctx", None),
            P("section", "exp", "ctx", None),
            P("section", "exp", "ctx", None),
            P("section", "ctx", None),
            P("section", None),
            P("section", "exp", None, "ctx"),
            P("section", "exp", None, "ctx"),
            P("section", "exp", None, "ctx"),
            P("section", "exp", "ctx", None),
            P("section", "exp", "ctx", None),
        ),
        out_specs=P("section", "exp", "ctx", None),
        check_vma=False,
    )
```

profile of v0, /device:TPU:1, one launch (start us, length us, event | category | flops | bytes accessed | tf_op | source)
XLA Modules:
  0.0 914.5 jit_solution(12395870145715200025)
XLA Ops:
  6.5 1.7 copy.21
  8.3 1.3 copy.13
  9.6 9.1 %all-to-all-start = ((bf16[128,8,512]{2,0,1:T(8,128)(2,1)}), bf16[128,8,512]{2,0,1:T(8,128)(2,1)S(1)}, u32[]{:S(2)}, u32[]{:S(2)}) async-start(bf16[128,8,512]{2,0,1:T(8,128)(2,1)} %copy.13), calls=%async_computation | async-start | bytes 2097152 | tf_op jit(solution)/shard_map/all_to_all | solution.py:51
  18.7 0.0 reduce-scatter.2.cloned.1.call-start
  18.8 39.9 %all-gather.1 = bf16[1,1,1024,256]{3,2,1,0:T(8,128)(2,1)S(1)} all-gather(bf16[1,1,128,256]{3,2,1,0:T(8,128)(2,1)S(1)} %copy-done.3), channel_id=3, replica_groups=mesh['section'=4,'ctx'=8,'exp'=8] {'ctx'}, dimensions={2}, use_global_device_ids=true | all-gather | bytes 589824 | tf_op jit(solution)/shard_map/all_gather | solution.py:54
  58.8 0.1 copy.14
  58.9 19.5 %all-gather = bf16[1,1,1024,256]{3,2,1,0:T(8,128)(2,1)S(1)} all-gather(bf16[1,1,128,256]{3,2,1,0:T(8,128)(2,1)S(1)} %copy-done.4), channel_id=2, replica_groups=mesh['section'=4,'ctx'=8,'exp'=8] {'ctx'}, dimensions={2}, use_global_device_ids=true | all-gather | bytes 589824 | tf_op jit(solution)/shard_map/all_gather | solution.py:53
  78.5 1.2 reshape.86
  79.7 28.7 %while.11 = (s32[]{:T(128)}, bf16[2,512,512]{2,1,0:T(8,128)(2,1)}, s32[2]{0:T(128)S(1)}, bf16[2,512,4,128]{3,2,1,0:T(4,128)(2,1)}, bf16[1024,128]{1,0:T(8,128)(2...) while((s32[]{:T(128)}, bf16[2,512,512]{2,1,0:T(8,128)(2,1)}, s32[2]{0:T(128)S(1)}, ...), condition=%wide.region_3.4_spmd.clone, body=%wide.region_0.3_spmd.clone.sunk | while | flops 1087112704 | bytes 22564972 | solution.py:80
  79.7 0.7 dynamic_slice.22
  80.4 0.7 iota_add_fusion.2
  81.1 0.4 iota_compare_fusion.6
  81.4 1.2 constant_dynamic-slice_fusion.3
  82.7 5.4 fusion.60
  88.0 5.0 fusion.61
  93.0 0.2 copy.36
  93.2 0.8 constant_dynamic-update-slice_fusion.2
  94.1 0.7 dynamic_slice.22
  94.7 0.7 iota_add_fusion.2
  95.4 0.4 iota_compare_fusion.6
  95.8 1.2 constant_dynamic-slice_fusion.3
  97.0 5.4 fusion.60
  102.4 5.0 fusion.61
  107.4 0.2 copy.36
  107.6 0.8 constant_dynamic-update-slice_fusion.2
  108.4 10.2 %convolution_convert_fusion.1 = bf16[1024,4096]{1,0:T(8,128)(2,1)} fusion(bf16[1024,512]{1,0:T(8,128)(2,1)} %bitcast.111, bf16[1,512,4096]{2,1,0:T(8,128)(2,1)} %param.17), kind=kOutput, calls=%fused_computation.26 | convolution fusion | flops 4299161600 | bytes 13631488 | tf_op jit(solution)/shard_map/dot_general | solution.py:84
  118.7 0.0 reduce-scatter.2.cloned.1.call-update
  118.7 0.7 copy-done.5
  119.4 0.1 fusion.41
  119.5 0.2 reduce_window_sum.11
  119.7 0.2 select_reduce_fusion
  119.9 105.6 %reduce-scatter.2.cloned.1.call-done = bf16[128,4096]{1,0:T(8,128)(2,1)} async-done(((bf16[1024,4096]{1,0:T(8,128)(2,1)}), bf16[128,4096]{1,0:T(8,128)(2,1)}) %reduce-scatter.2.cloned.1.call-update) | async-done | bytes 1048592 | tf_op jit(solution)/shard_map/reduce_scatter | solution.py:83
  225.5 1.7 multiply_reduce_fusion
  227.3 1.7 convolution_convert_fusion.2
  229.0 2.4 broadcast_in_dim.28
  231.4 7.6 broadcast_in_dim.38
  239.0 282.5 %all_to_all.25 = bf16[64,20,4096]{2,1,0:T(8,128)(2,1)} all-to-all(bf16[64,20,4096]{2,1,0:T(8,128)(2,1)} %bitcast.100), channel_id=1, replica_groups=mesh['section'=4,'ctx'=8,'exp'=8] {'ctx','exp'}, dimensions={0} | all-to-all | bytes 20971520 | tf_op jit(solution)/shard_map/all_to_all | solution.py:116
  521.4 14.2 %reshape.89 = bf16[1280,4096]{1,0:T(8,128)(2,1)} reshape(bf16[64,20,4096]{2,1,0:T(8,128)(2,1)} %all_to_all.25) | data formatting | bytes 20971520 | tf_op jit(solution)/shard_map/reshape | solution.py:117
  535.6 8.9 fusion.28
  544.5 19.0 %convolution_convert_fusion = bf16[1280,4096]{1,0:T(8,128)(2,1)} fusion(bf16[1,1,4096,192]{2,3,1,0:T(8,128)(2,1)S(1)} %copy-done, bf16[1280,4096]{1,0:T(8,128)(2,1)} %reshape.89, bf16[1,1,4096,192]{2,3,1,0:T(8,128)(2,1)} %param.20, f32[1280,192]{0,1:T(8,128)} %fusion.28), kind=kOutput, calls=%fused_computation.25 | convolution fusion | flops 4033249280 | bytes 25100288 | tf_op jit(solution)/shard_map/dot_general | solution.py:26
  563.5 13.9 %reshape.90 = bf16[64,20,4096]{2,1,0:T(8,128)(2,1)} reshape(bf16[1280,4096]{1,0:T(8,128)(2,1)} %convolution_convert_fusion) | data formatting | bytes 20971520 | tf_op jit(solution)/shard_map/reshape | solution.py:122
  577.5 281.7 %all_to_all.26 = bf16[64,20,4096]{2,1,0:T(8,128)(2,1)} all-to-all(bf16[64,20,4096]{2,1,0:T(8,128)(2,1)} %reshape.90), channel_id=1, replica_groups=mesh['section'=4,'ctx'=8,'exp'=8] {'ctx','exp'}, dimensions={0} | all-to-all | bytes 20971520 | tf_op jit(solution)/shard_map/all_to_all | solution.py:121
  859.2 14.2 %reshape.91 = bf16[8,160,4096]{2,1,0:T(8,128)(2,1)} reshape(bf16[64,20,4096]{2,1,0:T(8,128)(2,1)} %all_to_all.26) | data formatting | bytes 20971520 | tf_op jit(solution)/shard_map/reshape | solution.py:129
  873.4 7.3 reduce_sum.45
  880.7 2.2 fusion.23
  882.9 1.3 collective-permute-start
  884.2 22.4 %collective-permute-done = bf16[128,4096]{1,0:T(8,128)(2,1)S(1)} collective-permute-done((bf16[128,4096]{1,0:T(8,128)(2,1)S(1)}, bf16[128,4096]{1,0:T(8,128)(2,1)S(1)}, u32[]{:S(2)}, u32[]{:S(2)}) %collective-permute-start) | collective-permute-done | bytes 1048608 | tf_op jit(solution)/shard_map/ppermute | solution.py:16
  906.7 1.0 copy.45
  (23 shorter events, 0.1 us)
Async XLA Ops:
  6.5 538.0 %copy-start = (bf16[1,1,4096,192]{2,3,1,0:T(8,128)(2,1)S(1)}, bf16[1,1,4096,192]{2,3,1,0:T(8,128)(2,1)}, u32[]{:S(2)}) copy-start(bf16[1,1,4096,192]{2,3,1,0:T(8,128)(2,1)} %param.21) | copy-start | bytes 4718596
  8.3 10.5 %copy-start.3 = (bf16[1,1,128,256]{3,2,1,0:T(8,128)(2,1)S(1)}, bf16[1,1,128,256]{3,2,1,0:T(8,128)(2,1)}, u32[]{:S(2)}) copy-start(bf16[1,1,128,256]{3,2,1,0:T(8,128)(2,1)} %param.16) | copy-start | bytes 196612
  9.6 49.3 %copy-start.4 = (bf16[1,1,128,256]{3,2,1,0:T(8,128)(2,1)S(1)}, bf16[1,1,128,256]{3,2,1,0:T(8,128)(2,1)}, u32[]{:S(2)}) copy-start(bf16[1,1,128,256]{3,2,1,0:T(8,128)(2,1)} %param.15) | copy-start | bytes 196612
  9.6 68.9 %all-to-all-start = ((bf16[128,8,512]{2,0,1:T(8,128)(2,1)}), bf16[128,8,512]{2,0,1:T(8,128)(2,1)S(1)}, u32[]{:S(2)}, u32[]{:S(2)}) async-start(bf16[128,8,512]{2,0,1:T(8,128)(2,1)} %copy.13), calls=%async_computation | async-start | bytes 2097152 | tf_op jit(solution)/shard_map/all_to_all | solution.py:51
  18.7 206.8 %reduce-scatter.2.cloned.1.call-start = ((), (), s32[]{:S(2)}) async-start(), calls=%async_computation.4 | async-start | bytes 9437184 | tf_op jit(solution)/shard_map/reduce_scatter | solution.py:83
  118.7 0.7 copy-start.5
  118.7 0.7 copy-start.6
  118.7 106.8 %copy-start.1 = (bf16[1,1,128,4096]{3,2,1,0:T(8,128)(2,1)S(1)}, bf16[1,1,128,4096]{3,2,1,0:T(8,128)(2,1)}, u32[]{:S(2)}) copy-start(bf16[1,1,128,4096]{3,2,1,0:T(8,128)(2,1)} %param.13) | copy-start | bytes 3145732
  225.5 1.7 copy-start.2
  873.4 7.3 copy-start.7
  882.9 23.7 %collective-permute-start = (bf16[128,4096]{1,0:T(8,128)(2,1)S(1)}, bf16[128,4096]{1,0:T(8,128)(2,1)S(1)}, u32[]{:S(2)}, u32[]{:S(2)}) collective-permute-start(bf16[128,4096]{1,0:T(8,128)(2,1)S(1)} %fusion.23), channel_id=1, source_target_pairs={{0,64},{64,128},{128,192},{192,0},{1,65},{65,129},{129,193},{193,1... | collective-permute-start | bytes 3145736 | tf_op jit(solution)/shard_map/ppermute | solution.py:16
Sparse Core Ops, SparseCore 0:
  118.8 106.6 reduce-scatter.1
where the time goes:
time: 918 us; the launch traced here: 914 us
  blocking collectives  624 us (68%)
  waiting for transfers between devices  128 us (14%)
  local copies, waits for them, and re-layouts  64.3 us (7%)
  matrix products  62.8 us (7%)
  between operations  13.6 us (1%)
  other arithmetic  11.6 us (1%)
  starting transfers between devices  10.5 us (1%)
    all_to_all x1, blocking collectives, per_device(): lax.all_to_all(fanned, ('ctx', 'exp'), split_axis=0, concat_axis=0, tiled...  282 us
    all_to_all x1, blocking collectives, per_device(): lax.all_to_all(shard_out.reshape(ctx_count * exp_count, capacity, D), ('c...  282 us
    reduce_scatter x1, waiting for transfers between devices, per_device(): lax.psum_scatter(jnp.dot(attended, out_weight[0], preferred_element_type=...  106 us
    all_gather x1, blocking collectives, per_device(): lax.all_gather(values[0, 0], 'ctx', axis=0, tiled=True)  39.9 us
    ppermute x1, waiting for transfers between devices, passed_along(): lax.ppermute(array, axis, [(i, (i + by) % count) for i in range(count)])  22.4 us
    all_gather x1, blocking collectives, per_device(): lax.all_gather(keys[0, 0], 'ctx', axis=0, tiled=True)  19.5 us
    dot_general x1, matrix products, shrink_rows(): lax.dot_general(hidden, down_shard, (((1,), (1,)), ((), ())), preferred_e...  19 us
  transfers between devices with their start and end apart: 3, of which 2 were waited for; matrix products, arithmetic and copies ran while one was open for 0% of the time, Pallas kernels for 0%

commit v1 on v0

--- a/solution.py
+++ b/solution.py
@@ -1,9 +1,14 @@
+import functools
 import math
 
 import jax
 import jax.numpy as jnp
 from jax import lax
+from jax.experimental import pallas as pl
+from jax.experimental.pallas import tpu as pltpu
 from jax.sharding import PartitionSpec as P
+
+MESH = pl.DeviceIdType.MESH
 
 D = 4096
 QUERY_HEADS = 32
@@ -15,17 +20,233 @@
     count = lax.axis_size(axis)
     return lax.ppermute(array, axis, [(i, (i + by) % count) for i in range(count)])
 
-
-def expand_rows(rows_here, gate_shard, up_shard):
-    gate_part = jnp.dot(rows_here, gate_shard, preferred_element_type=jnp.float32)
-    up_part = jnp.dot(rows_here, up_shard, preferred_element_type=jnp.float32)
-    return (jax.nn.silu(gate_part) * up_part).astype(jnp.bfloat16)
-
-
-def shrink_rows(hidden, down_shard):
-    return lax.dot_general(
-        hidden, down_shard, (((1,), (1,)), ((), ())), preferred_element_type=jnp.float32
-    )
+def to_peer(axis, peer, src, dst, send_sem, recv_sem):
+    return pltpu.make_async_remote_copy(
+        src_ref=src,
+        dst_ref=dst,
+        send_sem=send_sem,
+        recv_sem=recv_sem,
+        device_id={axis: peer},
+        device_id_type=MESH,
+    )
+
+
+def greet(axis, me, n):
+    barrier = pltpu.get_barrier_semaphore()
+    for d in range(1, n):
+        pl.semaphore_signal(
+            barrier, inc=1, device_id={axis: lax.rem(me + d, n)}, device_id_type=MESH
+        )
+    pl.semaphore_wait(barrier, n - 1)
+
+
+def moe_kernel(
+    n,
+    mine,
+    gate_any,
+    up_any,
+    down_any,
+    out,
+    rows,
+    gate,
+    up,
+    down,
+    hid,
+    acc,
+    obuf,
+    load_sem,
+    rr_send,
+    rr_recv,
+    rl_send,
+    rl_recv,
+    hr_send,
+    hr_recv,
+    hl_send,
+    hl_recv,
+    wd_send,
+    wd_recv,
+    out_send,
+    out_recv,
+):
+    me = lax.axis_index("ctx")
+    right, left = lax.rem(me + 1, n), lax.rem(me + n - 1, n)
+    half = n // 2
+    count, width = mine.shape
+    part = out.shape[2]
+    units = gate.shape[1]
+    pair = count // 2
+    loads = [
+        pltpu.make_async_copy(gate_any, gate, load_sem.at[0]),
+        pltpu.make_async_copy(up_any, up, load_sem.at[1]),
+        pltpu.make_async_copy(
+            down_any.at[pl.ds(pl.multiple_of(me * part, part), part)], down.at[0], load_sem.at[2]
+        ),
+    ]
+    for load in loads:
+        load.start()
+    greet("ctx", me, n)
+
+    def slot(r):
+        return mine if r == 0 else rows.at[r]
+
+    def rows_step(s):
+        cut = width // 2
+        if s < half:
+            a = to_peer("ctx", right, slot((n + 1 - s) % n), rows.at[n - s], rr_send.at[s - 1], rr_recv.at[s - 1])
+            b = to_peer("ctx", left, slot(s - 1), rows.at[s], rl_send.at[s - 1], rl_recv.at[s - 1])
+        else:
+            a = to_peer(
+                "ctx", right, rows.at[n + 1 - s, :, pl.ds(0, cut)], rows.at[n - s, :, pl.ds(0, cut)], rr_send.at[s - 1], rr_recv.at[s - 1]
+            )
+            b = to_peer(
+                "ctx", left, rows.at[s - 1, :, pl.ds(cut, cut)], rows.at[s, :, pl.ds(cut, cut)], rl_send.at[s - 1], rl_recv.at[s - 1]
+            )
+        return a, b
+
+    def hid_step(s):
+        if s < half:
+            a = to_peer("ctx", right, hid.at[(n + 1 - s) % n], hid.at[n - s], hr_send.at[s - 1], hr_recv.at[s - 1])
+            b = to_peer("ctx", left, hid.at[s - 1], hid.at[s], hl_send.at[s - 1], hl_recv.at[s - 1])
+        else:
+            a = to_peer(
+                "ctx", right, hid.at[n + 1 - s, pl.ds(0, half)], hid.at[n - s, pl.ds(0, half)], hr_send.at[s - 1], hr_recv.at[s - 1]
+            )
+            b = to_peer(
+                "ctx", left, hid.at[s - 1, pl.ds(half, half)], hid.at[s, pl.ds(half, half)], hl_send.at[s - 1], hl_recv.at[s - 1]
+            )
+        return a, b
+
+    def expand(r):
+        block = slot(r)[...]
+        gate_part = jnp.dot(block, gate[...], preferred_element_type=jnp.float32)
+        up_part = jnp.dot(block, up[...], preferred_element_type=jnp.float32)
+        hidden = (gate_part / (1.0 + jnp.exp(-gate_part)) * up_part).astype(jnp.bfloat16)
+        owner = lax.rem(me + r, n)
+        hid[0, owner, 0:count, :] = hidden[:, 0:128]
+        hid[0, owner, count : count + pair, :] = jnp.concatenate(
+            [hidden[0:pair, 128:units], hidden[pair:count, 128:units]], axis=1
+        )
+
+    def shrink(r, b):
+        packed = hid[r, b]
+        tail = packed[count : count + pair]
+        rest = jnp.concatenate([tail[:, 0 : units - 128], tail[:, units - 128 :]], axis=0)
+        hidden = jnp.concatenate([packed[0:count], rest], axis=1)
+        return lax.dot_general(
+            hidden, down[r], (((1,), (1,)), ((), ())), preferred_element_type=jnp.float32
+        )
+
+    sent = list(rows_step(1))
+    for copy in sent:
+        copy.start()
+    downs = []
+    for d in (4, 3, 5, 2, 6, 1, 7):
+        peer = lax.rem(me + d, n)
+        downs.append(
+            to_peer(
+                "ctx",
+                peer,
+                down_any.at[pl.ds(pl.multiple_of(peer * part, part), part)],
+                down.at[n - d],
+                wd_send.at[d - 1],
+                wd_recv.at[n - d - 1],
+            )
+        )
+        downs[-1].start()
+    loads[0].wait()
+    loads[1].wait()
+    expand(0)
+    now = tuple(sent)
+    for s in range(1, half + 1):
+        for copy in now:
+            copy.wait_recv()
+        if s < half:
+            now = rows_step(s + 1)
+            for copy in now:
+                copy.start()
+            sent += now
+            expand(s)
+            expand(n - s)
+        else:
+            expand(s)
+    loads[2].wait()
+
+    now = hid_step(1)
+    sent += now
+    for copy in now:
+        copy.start()
+    for copy in downs:
+        copy.wait_recv()
+
+    @pl.loop(0, n)
+    def _(b):
+        acc[b] = shrink(0, b)
+
+    for s in range(1, half):
+        for copy in now:
+            copy.wait_recv()
+        now = hid_step(s + 1)
+        sent += now
+        for copy in now:
+            copy.start()
+
+        @pl.loop(0, n)
+        def _(b):
+            acc[b] += shrink(s, b) + shrink(n - s, b)
+
+    for copy in now:
+        copy.wait_recv()
+    for d in (4, 3, 5, 2, 6, 1, 7, 0):
+        b = lax.rem(me + d, n)
+        block = (acc[b] + shrink(half, b)).astype(jnp.bfloat16)
+        if d == 0:
+            out[b] = block
+        else:
+            obuf[d] = block
+            copy = to_peer("ctx", b, obuf.at[d], out.at[me], out_send.at[d], out_recv.at[n - d])
+            copy.start()
+            sent.append(copy)
+    for d in range(1, n):
+        source = lax.rem(me + d, n)
+        to_peer("ctx", source, obuf.at[d], out.at[source], out_send.at[d], out_recv.at[d]).wait_recv()
+    for copy in sent + downs:
+        copy.wait_send()
+
+
+def run_experts(mine, gate_shard, up_shard, down_shard):
+    n = lax.axis_size("ctx")
+    count, width = mine.shape
+    units = gate_shard.shape[1]
+    part = width // n
+    packed = count + count // 2
+    dma = pltpu.SemaphoreType.DMA
+    anywhere = pl.BlockSpec(memory_space=pl.ANY)
+    in_vmem = pl.BlockSpec(memory_space=pltpu.VMEM)
+    return pl.pallas_call(
+        functools.partial(moe_kernel, n),
+        out_shape=jax.ShapeDtypeStruct((n, count, part), jnp.bfloat16),
+        in_specs=[in_vmem, anywhere, anywhere, anywhere],
+        out_specs=in_vmem,
+        scratch_shapes=[
+            pltpu.VMEM((n, count, width), jnp.bfloat16),
+            pltpu.VMEM((width, units), jnp.bfloat16),
+            pltpu.VMEM((width, units), jnp.bfloat16),
+            pltpu.VMEM((n, part, units), jnp.bfloat16),
+            pltpu.VMEM((n, n, packed, 128), jnp.bfloat16),
+            pltpu.VMEM((n, count, part), jnp.float32),
+            pltpu.VMEM((n, count, part), jnp.bfloat16),
+            dma((3,)),
+        ]
+        + [dma((n // 2,))] * 8
+        + [dma((n - 1,))] * 2
+        + [dma((n,))] * 2,
+        compiler_params=pltpu.CompilerParams(
+            collective_id=0, has_side_effects=True, vmem_limit_bytes=48 * 2**20
+        ),
+        cost_estimate=pl.CostEstimate(
+            flops=6 * n * count * width * units, bytes_accessed=6 * width * units, transcendentals=0
+        ),
+    )(mine, gate_shard, up_shard, down_shard)
 
 
 def per_device(
@@ -110,24 +331,20 @@
     gate_shard = w_gate[0, 0]
     up_shard = w_up[0, 0]
     down_shard = w_down_t[0, 0]
-    fanned = jnp.broadcast_to(
-        outgoing.reshape(1, exp_count, capacity, D), (ctx_count, exp_count, capacity, D)
-    ).reshape(ctx_count * exp_count, capacity, D)
-    arrived = lax.all_to_all(fanned, ("ctx", "exp"), split_axis=0, concat_axis=0, tiled=True)
-    arrived_rows = arrived.reshape(ctx_count * exp_count * capacity, D)
-    shard_out = shrink_rows(expand_rows(arrived_rows, gate_shard, up_shard), down_shard).astype(
-        jnp.bfloat16
+    arrived = lax.all_to_all(
+        outgoing.reshape(exp_count, capacity, D), "exp", split_axis=0, concat_axis=0, tiled=True
+    )
+    finished = run_experts(
+        arrived.reshape(exp_count * capacity, D), gate_shard, up_shard, down_shard
     )
     returned = lax.all_to_all(
-        shard_out.reshape(ctx_count * exp_count, capacity, D),
-        ("ctx", "exp"),
+        finished.transpose(1, 0, 2).reshape(exp_count, capacity, D),
+        "exp",
         split_axis=0,
         concat_axis=0,
         tiled=True,
     )
-    expert_out = jnp.sum(
-        returned.reshape(ctx_count, exp_count * capacity, D), axis=0, dtype=jnp.float32
-    ).astype(jnp.bfloat16)
+    expert_out = returned.reshape(exp_count * capacity, D)
     routed = lax.dot_general(
         selector, expert_out, (((0,), (0,)), ((), ())), preferred_element_type=jnp.float32
     )

time: 918 us -> 535 us (0.58)
  blocking collectives: 624 us -> 88.2 us
  Pallas kernels: 0 us -> 216 us
  local copies, waits for them, and re-layouts: 64.3 us -> 23.2 us
  matrix products: 62.8 us -> 32.3 us
  waiting for transfers between devices: 128 us -> 143 us
    all_to_all x2 -> x1, blocking collectives: 564 us -> 28.7 us  [per_device(): lax.all_to_all(finished.transpose(1, 0, 2).reshape(exp_count, capacity, D...]
    pallas_call x0 -> x1, Pallas kernels: none -> 216 us  [run_experts(): pl.pallas_call(functools.partial(moe_kernel, n), out_shape=jax.ShapeDtype...]
    reshape x3 -> x4, local copies, waits for them, and re-layouts: 42.3 us -> 5.37 us  [the longest x1 1.67 us: per_device(): expert_out = returned.reshape(exp_count * capacity, D)]
    dot_general x2 -> x0, matrix products: 27.9 us -> none  [the longest x1 19 us: shrink_rows(): lax.dot_general(hidden, down_shard, (((1,), (1,)), ((), ())), preferred_e...]
    all_to_all x0 -> x1, waiting for transfers between devices: none -> 12.7 us  [per_device(): lax.all_to_all(outgoing.reshape(exp_count, capacity, D), 'exp', split_axi...]
    broadcast_in_dim x2 -> x0, local copies, waits for them, and re-layouts: 9.99 us -> none  [per_device(): jnp.broadcast_to(outgoing.reshape(1, exp_count, capacity, D), (ctx_count,...]
  transfers between devices with their start and end apart: 3 -> 4, of which waited for: 2 -> 3; matrix products, arithmetic and copies ran while one was open for 0% -> 2% of each run, Pallas kernels for 0% -> 0%
where the time goes in v1:
time: 535 us
  Pallas kernels  216 us (40%)
  waiting for transfers between devices  143 us (27%)
  blocking collectives  88.2 us (16%)
  matrix products  32.3 us (6%)
  local copies, waits for them, and re-layouts  23.2 us (4%)
  starting transfers between devices  14.9 us (3%)
  between operations  13.6 us (3%)
    pallas_call x1, Pallas kernels, run_experts(): pl.pallas_call(functools.partial(moe_kernel, n), out_shape=jax.ShapeDtype...  216 us
    reduce_scatter x1, waiting for transfers between devices, per_device(): lax.psum_scatter(jnp.dot(attended, out_weight[0], preferred_element_type=...  106 us
    all_gather x1, blocking collectives, per_device(): lax.all_gather(values[0, 0], 'ctx', axis=0, tiled=True)  39.9 us
    all_to_all x1, blocking collectives, per_device(): lax.all_to_all(finished.transpose(1, 0, 2).reshape(exp_count, capacity, D...  28.7 us
    ppermute x1, waiting for transfers between devices, passed_along(): lax.ppermute(array, axis, [(i, (i + by) % count) for i in range(count)])  24.2 us
    all_gather x1, blocking collectives, per_device(): lax.all_gather(keys[0, 0], 'ctx', axis=0, tiled=True)  19.5 us
    all_to_all x1, waiting for transfers between devices, per_device(): lax.all_to_all(outgoing.reshape(exp_count, capacity, D), 'exp', split_axi...  12.7 us
    unnamed x27, local copies, waits for them, and re-layouts  11.6 us
  transfers between devices with their start and end apart: 4, of which 3 were waited for; matrix products, arithmetic and copies ran while one was open for 2% of the time, Pallas kernels for 0%

profile of v1, /device:TPU:1, one launch (start us, length us, event | category | flops | bytes accessed | tf_op | source)
XLA Modules:
  0.0 534.8 jit_solution(7292515926777169682)
XLA Ops:
  6.5 1.6 copy.27
  8.2 1.3 copy.16
  9.4 9.1 %all-to-all-start = ((bf16[128,8,512]{2,0,1:T(8,128)(2,1)}), bf16[128,8,512]{2,0,1:T(8,128)(2,1)S(1)}, u32[]{:S(2)}, u32[]{:S(2)}) async-start(bf16[128,8,512]{2,0,1:T(8,128)(2,1)} %copy.16), calls=%async_computation | async-start | bytes 2097152 | tf_op jit(solution)/shard_map/all_to_all | solution.py:272
  18.7 39.9 %all-gather.1 = bf16[1,1,1024,256]{3,2,1,0:T(8,128)(2,1)S(1)} all-gather(bf16[1,1,128,256]{3,2,1,0:T(8,128)(2,1)S(1)} %copy-done.6), channel_id=3, replica_groups=mesh['section'=4,'ctx'=8,'exp'=8] {'ctx'}, dimensions={2}, use_global_device_ids=true | all-gather | bytes 589824 | tf_op jit(solution)/shard_map/all_gather | solution.py:275
  58.6 0.1 copy.17
  58.8 19.5 %all-gather = bf16[1,1,1024,256]{3,2,1,0:T(8,128)(2,1)S(1)} all-gather(bf16[1,1,128,256]{3,2,1,0:T(8,128)(2,1)S(1)} %copy-done.7), channel_id=2, replica_groups=mesh['section'=4,'ctx'=8,'exp'=8] {'ctx'}, dimensions={2}, use_global_device_ids=true | all-gather | bytes 589824 | tf_op jit(solution)/shard_map/all_gather | solution.py:274
  78.3 0.3 reshape.84
  78.6 26.4 %while.11 = (s32[]{:T(128)}, bf16[2,512,512]{2,1,0:T(8,128)(2,1)}, s32[2]{0:T(128)S(1)}, bf16[2,512,4,128]{3,2,1,0:T(4,128)(2,1)S(1)}, bf16[1024,128]{1,0:T(8,12...) while((s32[]{:T(128)}, bf16[2,512,512]{2,1,0:T(8,128)(2,1)}, s32[2]{0:T(128)S(1)}, ...), condition=%wide.region_3.4_spmd.clone, body=%wide.region_0.3_spmd.clone.sunk | while | flops 1087112704 | bytes 22565472 | solution.py:301
  78.7 0.6 dynamic_slice.22
  79.3 0.6 iota_add_fusion.2
  79.9 0.4 iota_compare_fusion.6
  80.3 0.2 constant_dynamic-slice_fusion.3
  80.5 5.4 %fusion.44 = (f32[4,512]{1,0:T(4,128)S(1)}, f32[4,512,1024]{2,1,0:T(8,128)}) fusion(pred[512,1024]{1,0:T(8,128)(4,1)S(1)} %iota_compare_fusion.6, bf16[1,512,4,128]{3,2,1,0:T(4,128)(2,1)S(1)} %constant_dynamic-slice_fusion.3, bf16[1024,128]{1,0:T(8,128)(2,1)S(1)} %get-tuple-element.136), kind=kOutput, calls=%fused_computation.48.clone.1 | convolution fusion | flops 545260544 | bytes 9707520 | tf_op jit(solution)/shard_map/while/body/eval_jaxpr/sub | solution.py:295
  85.8 5.0 fusion.45
  90.8 0.2 copy.42
  91.0 0.8 constant_dynamic-update-slice_fusion.2
  91.9 0.6 dynamic_slice.22
  92.5 0.6 iota_add_fusion.2
  93.1 0.4 iota_compare_fusion.6
  93.5 0.2 constant_dynamic-slice_fusion.3
  93.7 5.4 %fusion.44 = (f32[4,512]{1,0:T(4,128)S(1)}, f32[4,512,1024]{2,1,0:T(8,128)}) fusion(pred[512,1024]{1,0:T(8,128)(4,1)S(1)} %iota_compare_fusion.6, bf16[1,512,4,128]{3,2,1,0:T(4,128)(2,1)S(1)} %constant_dynamic-slice_fusion.3, bf16[1024,128]{1,0:T(8,128)(2,1)S(1)} %get-tuple-element.136), kind=kOutput, calls=%fused_computation.48.clone.1 | convolution fusion | flops 545260544 | bytes 9707520 | tf_op jit(solution)/shard_map/while/body/eval_jaxpr/sub | solution.py:295
  99.0 5.0 fusion.45
  104.0 0.2 copy.42
  104.2 0.8 constant_dynamic-update-slice_fusion.2
  105.1 10.2 %convolution_convert_fusion = bf16[1024,4096]{1,0:T(8,128)(2,1)} fusion(bf16[1024,512]{1,0:T(8,128)(2,1)} %bitcast.104, bf16[1,512,4096]{2,1,0:T(8,128)(2,1)} %param.17), kind=kOutput, calls=%fused_computation.25 | convolution fusion | flops 4299161600 | bytes 13631488 | tf_op jit(solution)/shard_map/dot_general | solution.py:305
  115.3 0.6 copy-done.9
  116.0 0.2 reduce_window_sum.11
  116.2 0.2 select_reduce_fusion
  116.4 105.7 %reduce-scatter.2.cloned.1.call-done = bf16[128,4096]{1,0:T(8,128)(2,1)} async-done(((bf16[1024,4096]{1,0:T(8,128)(2,1)}), bf16[128,4096]{1,0:T(8,128)(2,1)}) %reduce-scatter.2.cloned.1.call-update) | async-done | bytes 1048592 | tf_op jit(solution)/shard_map/reduce_scatter | solution.py:304
  222.1 1.8 multiply_reduce_fusion
  224.0 0.6 convolution_convert_fusion.1
  224.6 1.3 reshape.86
  226.0 5.0 all-to-all-start.1
  231.0 2.5 copy.21
  233.4 2.5 copy.22
  235.9 3.1 copy.20
  239.1 12.7 %all-to-all-done.1 = bf16[8,20,4096]{2,1,0:T(8,128)(2,1)} async-done(((bf16[8,20,4096]{2,1,0:T(8,128)(2,1)}), bf16[8,20,4096]{2,1,0:T(8,128)(2,1)}, u32[]{:S(2)}, u32[]{:S(2)}) %all-to-all-start.1) | async-done | bytes 1310752 | tf_op jit(solution)/shard_map/all_to_all | solution.py:334
  251.8 1.5 reshape.87.mine
  253.3 215.7 %shard_map.109 = bf16[8,160,512]{2,1,0:T(8,128)(2,1)S(1)} custom-call(bf16[160,4096]{1,0:T(8,128)(2,1)S(1)} %reshape.87.mine, bf16[4096,192]{1,0:T(8,128)(2,1)S(1)} %bitcast.90, bf16[4096,192]{1,0:T(8,128)(2,1)} %bitcast.95, bf16[4096,192]{1,0:T(8,128)(2,1)} %bitcast.96), custom_call_target="tpu_custom_call" | custom-call | flops 6039797760 | bytes 4718592 | tf_op jit(solution)/shard_map/pallas_call | solution.py:225
  469.0 0.7 copy.23
  469.8 0.8 reshape.88
  470.6 28.7 %all_to_all.25 = bf16[8,20,4096]{2,1,0:T(8,128)(2,1)} all-to-all(bf16[8,20,4096]{2,1,0:T(8,128)(2,1)S(1)} %reshape.88), channel_id=1, replica_groups=mesh['section'=4,'ctx'=8,'exp'=8] {'exp'}, dimensions={0} | all-to-all | bytes 2621440 | tf_op jit(solution)/shard_map/all_to_all | solution.py:340
  499.4 1.7 reshape.89
  501.0 0.3 copy-done.3
  501.4 0.7 fusion.23
  502.1 0.7 collective-permute-start
  502.8 24.2 %collective-permute-done = bf16[128,4096]{1,0:T(8,128)(2,1)S(1)} collective-permute-done((bf16[128,4096]{1,0:T(8,128)(2,1)S(1)}, bf16[128,4096]{1,0:T(8,128)(2,1)S(1)}, u32[]{:S(2)}, u32[]{:S(2)}) %collective-permute-start) | collective-permute-done | bytes 1048608 | tf_op jit(solution)/shard_map/ppermute | solution.py:21
  527.0 1.0 copy.51
  (31 shorter events, 0.3 us)
Async XLA Ops:
  8.2 10.5 %copy-start.6 = (bf16[1,1,128,256]{3,2,1,0:T(8,128)(2,1)S(1)}, bf16[1,1,128,256]{3,2,1,0:T(8,128)(2,1)}, u32[]{:S(2)}) copy-start(bf16[1,1,128,256]{3,2,1,0:T(8,128)(2,1)} %param.16) | copy-start | bytes 196612
  9.4 49.3 %copy-start.7 = (bf16[1,1,128,256]{3,2,1,0:T(8,128)(2,1)S(1)}, bf16[1,1,128,256]{3,2,1,0:T(8,128)(2,1)}, u32[]{:S(2)}) copy-start(bf16[1,1,128,256]{3,2,1,0:T(8,128)(2,1)} %param.15) | copy-start | bytes 196612
  9.4 68.9 %all-to-all-start = ((bf16[128,8,512]{2,0,1:T(8,128)(2,1)}), bf16[128,8,512]{2,0,1:T(8,128)(2,1)S(1)}, u32[]{:S(2)}, u32[]{:S(2)}) async-start(bf16[128,8,512]{2,0,1:T(8,128)(2,1)} %copy.16), calls=%async_computation | async-start | bytes 2097152 | tf_op jit(solution)/shard_map/all_to_all | solution.py:272
  18.6 203.5 %reduce-scatter.2.cloned.1.call-start = ((), (), s32[]{:S(2)}) async-start(), calls=%async_computation.4 | async-start | bytes 9437184 | tf_op jit(solution)/shard_map/reduce_scatter | solution.py:304
  115.3 0.7 copy-start.9
  115.3 0.9 copy-start.8
  115.3 106.8 %copy-start = (bf16[1,1,128,4096]{3,2,1,0:T(8,128)(2,1)S(1)}, bf16[1,1,128,4096]{3,2,1,0:T(8,128)(2,1)}, u32[]{:S(2)}) copy-start(bf16[1,1,128,4096]{3,2,1,0:T(8,128)(2,1)} %param.13) | copy-start | bytes 3145732
  222.1 1.9 copy-start.2
  226.0 5.0 copy-start.4
  226.0 25.8 %all-to-all-start.1 = ((bf16[8,20,4096]{2,1,0:T(8,128)(2,1)}), bf16[8,20,4096]{2,1,0:T(8,128)(2,1)}, u32[]{:S(2)}, u32[]{:S(2)}) async-start(bf16[8,20,4096]{2,1,0:T(8,128)(2,1)} %reshape.86), calls=%async_computation.2 | async-start | bytes 3145728 | tf_op jit(solution)/shard_map/all_to_all | solution.py:334
  231.0 2.5 copy-start.5
  499.3 1.7 copy-start.1
  499.3 2.0 copy-start.3
  499.4 2.0 copy-start.10
  502.1 24.9 %collective-permute-start = (bf16[128,4096]{1,0:T(8,128)(2,1)S(1)}, bf16[128,4096]{1,0:T(8,128)(2,1)S(1)}, u32[]{:S(2)}, u32[]{:S(2)}) collective-permute-start(bf16[128,4096]{1,0:T(8,128)(2,1)S(1)} %fusion.23), channel_id=1, source_target_pairs={{0,64},{64,128},{128,192},{192,0},{1,65},{65,129},{129,193},{193,1... | collective-permute-start | bytes 3145736 | tf_op jit(solution)/shard_map/ppermute | solution.py:21
Sparse Core Ops, SparseCore 0:
  115.5 106.6 reduce-scatter.1

commit v2 on v1

v2 whole, which is shorter than its diff:
```python
import functools
import math

import jax
import jax.numpy as jnp
from jax import lax
from jax.experimental import pallas as pl
from jax.experimental.pallas import tpu as pltpu
from jax.sharding import PartitionSpec as P

D = 4096
QUERY_HEADS = 32
KEY_VALUE_HEADS = 2
HEAD_SIZE = 128
CORES = 2
MESH = pl.DeviceIdType.MESH
BF16, F32, I32 = jnp.bfloat16, jnp.float32, jnp.int32


def to_peer(peer, src, dst, send_sem, recv_sem):
    return pltpu.make_async_remote_copy(
        src_ref=src,
        dst_ref=dst,
        send_sem=send_sem,
        recv_sem=recv_sem,
        device_id=peer,
        device_id_type=MESH,
    )


def greet(peers):
    barrier = pltpu.get_barrier_semaphore()
    for peer in peers:
        pl.semaphore_signal(barrier, inc=1, device_id=peer, device_id_type=MESH)
    pl.semaphore_wait(barrier, len(peers))


def lanes(start, size):
    return pl.ds(pl.multiple_of(start, 128), size)


def across(a, b):
    return lax.dot_general(a, b, (((1,), (1,)), ((), ())), preferred_element_type=F32)


def passed_along(array, axis, by):
    count = lax.axis_size(axis)
    return lax.ppermute(array, axis, [(i, (i + by) % count) for i in range(count)])


def attend_kernel(
    n,
    cols,
    capacity,
    query,
    kv_in,
    ids_in,
    gates_in,
    gain,
    hidden_any,
    weight_any,
    down_any,
    residual,
    mine,
    slots,
    gates,
    down,
    kv,
    mixed,
    weight,
    hidden,
    ids,
    squares,
    bias,
    outgoing,
    local_sem,
    kr_send,
    kr_recv,
    kl_send,
    kl_recv,
    wr_send,
    wr_recv,
    wl_send,
    wl_recv,
    sib_send,
    sib_recv,
    x_send,
    x_recv,
    small_send,
    small_recv,
    sq_send,
    sq_recv,
    out_send,
    out_recv,
    wd_send,
    wd_recv,
):
    z = lax.axis_index("ctx")
    me = lax.axis_index("exp")
    x, core = me // CORES, lax.rem(me, CORES)
    experts = cols * CORES
    half = n // 2
    tokens = query.shape[0]
    width = query.shape[1]
    wide = width // cols
    chunk = width // n
    part = width // n
    heads = chunk // HEAD_SIZE
    group = QUERY_HEADS // KEY_VALUE_HEADS // heads
    up, below = {"ctx": lax.rem(z + 1, n)}, {"ctx": lax.rem(z + n - 1, n)}
    col = [lax.rem(x + d, cols) for d in range(cols)]
    same = [{"exp": col[d] * CORES + core} for d in range(cols)]
    sibling = {"exp": x * CORES + 1 - core}

    locals_ = [
        pltpu.make_async_copy(kv_in, kv.at[z], local_sem.at[0]),
        pltpu.make_async_copy(
            weight_any.at[:, lanes(x * wide, chunk)], weight.at[z, 0], local_sem.at[1]
        ),
        pltpu.make_async_copy(
            weight_any.at[:, lanes(x * wide + chunk, chunk)], weight.at[z, 1], local_sem.at[2]
        ),
        pltpu.make_async_copy(hidden_any.at[:, lanes(x * wide, wide)], hidden.at[x], local_sem.at[3]),
        pltpu.make_async_copy(ids_in, ids.at[x], local_sem.at[4]),
        pltpu.make_async_copy(gates_in, gates.at[x], local_sem.at[5]),
        pltpu.make_async_copy(down_any.at[:, lanes(z * part, part)], down.at[0], local_sem.at[6]),
    ]
    for copy in locals_:
        copy.start()
    greet(
        [{"ctx": lax.rem(z + d, n)} for d in range(1, n)]
        + [{"exp": lax.rem(me + d, experts)} for d in range(1, experts)]
    )

    def kv_step(s):
        a, b = lax.rem(z + n + 1 - s, n), lax.rem(z + s - 1, n)
        cut = tokens // 2
        one, two = kv.at[a], kv.at[b]
        if s == half:
            one, two = kv.at[a, pl.ds(0, cut)], kv.at[b, pl.ds(cut, cut)]
        return (
            to_peer(up, kv_in if s == 1 else one, one, kr_send.at[s - 1], kr_recv.at[s - 1]),
            to_peer(below, kv_in if s == 1 else two, two, kl_send.at[s - 1], kl_recv.at[s - 1]),
        )

    def weight_step(s):
        a, b = lax.rem(z + n + 1 - s, n), lax.rem(z + s - 1, n)
        cut = chunk // 2
        one, two = weight.at[a, core], weight.at[b, core]
        if s == half:
            one, two = weight.at[a, core, pl.ds(0, cut)], weight.at[b, core, pl.ds(cut, cut)]
        own = weight_any.at[:, lanes(x * wide + core * chunk, chunk)]
        return (
            to_peer(up, own if s == 1 else one, one, wr_send.at[s - 1], wr_recv.at[s - 1]),
            to_peer(below, own if s == 1 else two, two, wl_send.at[s - 1], wl_recv.at[s - 1]),
        )

    def share(off):
        k = lax.rem(z + off, n)
        return to_peer(
            sibling, weight.at[k, core], weight.at[k, core], sib_send.at[off], sib_recv.at[off]
        )

    def shared(off):
        k = lax.rem(z + off, n)
        return to_peer(
            sibling, weight.at[k, 1 - core], weight.at[k, 1 - core], sib_send.at[off], sib_recv.at[off]
        )

    def weight_arrived(s):
        for copy in weight_step(s):
            copy.wait_recv()
        if s < half:
            for copy in weight_step(s + 1):
                copy.start()
            share(n - s).start()
        share(s).start()

    small = []
    for d in range(1, cols):
        for at, (src, dst) in enumerate(
            (
                (ids_in, ids.at[x]),
                (gates_in, gates.at[x]),
                (hidden_any.at[:, lanes(col[d] * wide, wide)], hidden.at[x]),
            )
        ):
            small.append(
                to_peer(same[d], src, dst, small_send.at[d, at], small_recv.at[cols - d, at])
            )
    now = kv_step(1)
    for copy in now:
        copy.start()
    for copy in small:
        copy.start()

    row = lax.broadcasted_iota(I32, (tokens, n * tokens), 0) + z * tokens
    column = lax.broadcasted_iota(I32, (tokens, n * tokens), 1)
    bias[...] = jnp.where(row >= column, 0.0, -1e30)
    residual[...] = jnp.zeros_like(residual)

    for s in range(1, half + 1):
        for copy in now:
            copy.wait_recv()
        if s < half:
            now = kv_step(s + 1)
            for copy in now:
                copy.start()
    for copy in weight_step(1):
        copy.start()
    locals_[0].wait()

    def place(j):
        odd = lax.rem(j, 2)
        off = odd * ((j + 1) // 2) + (1 - odd) * lax.rem(n - j // 2, n)
        return off, lax.rem(z + off, n)

    def chunk_first(j):
        _, k = place(j)
        return (
            to_peer(same[1], mixed.at[k, x], mixed.at[k, x], x_send.at[j, 0], x_recv.at[j, 0]),
            to_peer(same[cols - 1], mixed.at[k, x], mixed.at[k, x], x_send.at[j, 1], x_recv.at[j, 1]),
        )

    def chunk_second(j):
        _, k = place(j)
        cut = tokens // 2
        one = mixed.at[k, col[cols - 1], pl.ds(0, cut)]
        two = mixed.at[k, col[1], pl.ds(cut, cut)]
        return (
            to_peer(same[1], one, one, x_send.at[j, 2], x_recv.at[j, 2]),
            to_peer(same[cols - 1], two, two, x_send.at[j, 3], x_recv.at[j, 3]),
        )

    def chunk_forward(j):
        for copy in chunk_first(j):
            copy.wait_recv()
        for copy in chunk_second(j):
            copy.start()

    def project(j):
        off, k = place(j)
        for copy in chunk_second(j):
            copy.wait_recv()

        @pl.when(off > 0)
        def _():
            shared(off).wait_recv()

        rows = mixed[k].reshape(cols * tokens, chunk)
        for side in range(CORES):
            residual[:, side * chunk : (side + 1) * chunk] += jnp.dot(
                rows, weight[k, side], preferred_element_type=F32
            )

    scale = math.log2(math.e) / math.sqrt(HEAD_SIZE)

    @pl.loop(0, n)
    def _(j):
        _, k = place(j)
        kv_head = k // group
        key = kv[:, :, lanes(kv_head * HEAD_SIZE, HEAD_SIZE)].reshape(n * tokens, HEAD_SIZE)
        value = kv[
            :, :, lanes((KEY_VALUE_HEADS + kv_head) * HEAD_SIZE, HEAD_SIZE)
        ].reshape(n * tokens, HEAD_SIZE)
        for h in range(heads):
            scores = across(query[:, lanes(k * chunk + h * HEAD_SIZE, HEAD_SIZE)], key) + bias[...]
            top = jnp.max(scores, axis=-1, keepdims=True)
            shifted = jnp.exp2((scores - top) * scale)
            total = jnp.sum(shifted, axis=-1, keepdims=True)
            out = jnp.dot(shifted.astype(BF16), value, preferred_element_type=F32)
            mixed[k, x, :, h * HEAD_SIZE : (h + 1) * HEAD_SIZE] = (out / total).astype(BF16)
        for copy in chunk_first(j):
            copy.start()

        @pl.when(j >= 1)
        def _():
            chunk_forward(j - 1)

        @pl.when(j == 2)
        def _():
            locals_[1].wait()
            locals_[2].wait()
            weight_arrived(1)

        @pl.when(j == 5)
        def _():
            weight_arrived(2)

        @pl.when(j >= 3)
        def _():
            project(j - 3)

    chunk_forward(n - 1)
    weight_arrived(3)
    project(n - 3)
    project(n - 2)
    weight_arrived(4)
    downs = []
    for d in (4, 3, 5, 2, 6, 1, 7):
        peer = lax.rem(z + d, n)
        downs.append(
            to_peer(
                {"ctx": peer},
                down_any.at[:, lanes(peer * part, part)],
                down.at[n - d],
                wd_send.at[d],
                wd_recv.at[n - d],
            )
        )
        downs[-1].start()
    for copy in small:
        copy.wait_recv()
    for copy in locals_[3:]:
        copy.wait()

    expert = lax.broadcasted_iota(I32, (experts, tokens), 0)
    earlier = lax.broadcasted_iota(I32, (tokens, tokens), 0) < lax.broadcasted_iota(
        I32, (tokens, tokens), 1
    )
    earlier = jnp.where(earlier, 1.0, 0.0).astype(BF16)
    placed = []
    for q in range(cols):
        chosen = ids[q]
        named = jnp.where(expert == chosen, 1.0, 0.0)
        before = jnp.dot(named.astype(BF16), earlier, preferred_element_type=F32)
        rank = jnp.sum(before * named, axis=0, keepdims=True)
        placed.append(
            chosen[0:1] * (cols * capacity) + q * capacity + rank.astype(I32)
        )
    placed = jnp.concatenate(placed, axis=1)
    slots[...] = jnp.broadcast_to(placed, slots.shape)
    slot = lax.broadcasted_iota(I32, (experts * cols * capacity, cols * tokens), 0)
    selector = jnp.where(slot == placed, 1.0, 0.0).astype(BF16)

    project(n - 1)
    residual[...] += hidden[...].reshape(cols * tokens, wide).astype(F32)
    res = residual[...]
    squares[x] = lax.dot_general(
        jnp.ones((8, wide), F32),
        res * res,
        (((1,), (1,)), ((), ())),
        precision=lax.Precision.HIGHEST,
        preferred_element_type=F32,
    )
    sums = [
        to_peer(same[d], squares.at[x], squares.at[x], sq_send.at[d], sq_recv.at[cols - d])
        for d in range(1, cols)
    ]
    for copy in sums:
        copy.start()
    for copy in sums:
        copy.wait_recv()
    total = squares[0]
    for q in range(1, cols):
        total += squares[q]
    inverse = jnp.transpose(lax.rsqrt(total * (1.0 / width) + 1e-06))[:, 0:1]
    normed = (res * inverse * gain[:, lanes(x * wide, wide)].astype(F32)).astype(BF16)
    rows = cols * capacity
    picked = jnp.dot(selector, normed, preferred_element_type=F32).astype(BF16)
    outgoing[...] = picked.reshape(experts, rows, wide)
    sent = []
    for d in (4, 5, 2, 6, 3, 7, 1):
        e = lax.rem(me + d, experts)
        sent.append(
            to_peer(
                {"exp": e},
                outgoing.at[e],
                mine.at[core, :, lanes(x * wide, wide)],
                out_send.at[d],
                out_recv.at[experts - d],
            )
        )
        sent[-1].start()
    keep = pltpu.make_async_copy(
        outgoing.at[me], mine.at[core, :, lanes(x * wide, wide)], local_sem.at[0]
    )
    keep.start()
    keep.wait()
    for copy in sent:
        copy.wait_recv()
    for copy in downs:
        copy.wait_recv()

    for copy in small + sums + sent + downs:
        copy.wait_send()
    for s in range(1, half + 1):
        for copy in kv_step(s) + weight_step(s):
            copy.wait_send()
    for off in range(1, n):
        share(off).wait_send()

    @pl.loop(0, n)
    def _(j):
        for copy in chunk_first(j) + chunk_second(j):
            copy.wait_send()


def run_attend(query, kv, ids, gates, gain, hidden, weight, down, capacity):
    n = lax.axis_size("ctx")
    experts = lax.axis_size("exp")
    cols = experts // CORES
    tokens, width = query.shape
    wide, part = width // cols, width // n
    units = down.shape[0]
    dma = pltpu.SemaphoreType.DMA
    anywhere = pl.BlockSpec(memory_space=pl.ANY)
    in_vmem = pl.BlockSpec(memory_space=pltpu.VMEM)
    shape = jax.ShapeDtypeStruct
    return pl.pallas_call(
        functools.partial(attend_kernel, n, cols, capacity),
        out_shape=(
            shape((cols * tokens, wide), F32),
            shape((CORES, cols * capacity, width), BF16),
            shape((8, cols * tokens), I32),
            shape((cols, tokens, 128), F32),
            shape((n, units, part), BF16),
        ),
        in_specs=[in_vmem] * 5 + [anywhere] * 3,
        out_specs=(in_vmem,) * 5,
        scratch_shapes=[
            pltpu.VMEM((n, tokens, kv.shape[1]), BF16),
            pltpu.VMEM((n, cols, tokens, width // n), BF16),
            pltpu.VMEM((n, CORES, width // n, width // n), BF16),
            pltpu.VMEM((cols, tokens, wide), BF16),
            pltpu.VMEM((cols, 8, tokens), I32),
            pltpu.VMEM((cols, 8, cols * tokens), F32),
            pltpu.VMEM((tokens, n * tokens), F32),
            pltpu.VMEM((experts, cols * capacity, wide), BF16),
            dma((7,)),
        ]
        + [dma((n // 2,))] * 8
        + [dma((n,))] * 2
        + [dma((n, 4))] * 2
        + [dma((cols, 3))] * 2
        + [dma((cols,))] * 2
        + [dma((experts,))] * 2
        + [dma((n,))] * 2,
        compiler_params=pltpu.CompilerParams(
            collective_id=1, has_side_effects=True, vmem_limit_bytes=56 * 2**20
        ),
        cost_estimate=pl.CostEstimate(
            flops=2 * cols * tokens * width * wide,
            bytes_accessed=8 * 2**20,
            transcendentals=QUERY_HEADS * tokens * n * tokens,
        ),
    )(query, kv, ids, gates, gain, hidden, weight, down)


def moe_kernel(
    n,
    mine,
    down,
    gate_any,
    up_any,
    out,
    rows,
    gate,
    up,
    hid,
    acc,
    obuf,
    load_sem,
    rr_send,
    rr_recv,
    rl_send,
    rl_recv,
    hr_send,
    hr_recv,
    hl_send,
    hl_recv,
    out_send,
    out_recv,
):
    me = lax.axis_index("ctx")
    right, left = {"ctx": lax.rem(me + 1, n)}, {"ctx": lax.rem(me + n - 1, n)}
    half = n // 2
    count, width = mine.shape
    units = gate.shape[0]
    pair = count // 2
    loads = [
        pltpu.make_async_copy(gate_any, gate, load_sem.at[0]),
        pltpu.make_async_copy(up_any, up, load_sem.at[1]),
    ]
    for load in loads:
        load.start()
    greet([{"ctx": lax.rem(me + d, n)} for d in range(1, n)])

    def slot(r):
        return mine if r == 0 else rows.at[r]

    def rows_step(s):
        cut = width // 2
        if s < half:
            a = to_peer(right, slot((n + 1 - s) % n), rows.at[n - s], rr_send.at[s - 1], rr_recv.at[s - 1])
            b = to_peer(left, slot(s - 1), rows.at[s], rl_send.at[s - 1], rl_recv.at[s - 1])
        else:
            a = to_peer(
                right, rows.at[n + 1 - s, :, pl.ds(0, cut)], rows.at[n - s, :, pl.ds(0, cut)], rr_send.at[s - 1], rr_recv.at[s - 1]
            )
            b = to_peer(
                left, rows.at[s - 1, :, pl.ds(cut, cut)], rows.at[s, :, pl.ds(cut, cut)], rl_send.at[s - 1], rl_recv.at[s - 1]
            )
        return a, b

    def hid_step(s):
        if s < half:
            a = to_peer(right, hid.at[(n + 1 - s) % n], hid.at[n - s], hr_send.at[s - 1], hr_recv.at[s - 1])
            b = to_peer(left, hid.at[s - 1], hid.at[s], hl_send.at[s - 1], hl_recv.at[s - 1])
        else:
            a = to_peer(
                right, hid.at[n + 1 - s, pl.ds(0, half)], hid.at[n - s, pl.ds(0, half)], hr_send.at[s - 1], hr_recv.at[s - 1]
            )
            b = to_peer(
                left, hid.at[s - 1, pl.ds(half, half)], hid.at[s, pl.ds(half, half)], hl_send.at[s - 1], hl_recv.at[s - 1]
            )
        return a, b

    def expand(r):
        block = slot(r)[...]
        gate_part = across(block, gate[...])
        up_part = across(block, up[...])
        hidden = (gate_part / (1.0 + jnp.exp(-gate_part)) * up_part).astype(BF16)
        owner = lax.rem(me + r, n)
        hid[0, owner, 0:count, :] = hidden[:, 0:128]
        hid[0, owner, count : count + pair, :] = jnp.concatenate(
            [hidden[0:pair, 128:units], hidden[pair:count, 128:units]], axis=1
        )

    def shrink(r, b):
        packed = hid[r, b]
        tail = packed[count : count + pair]
        rest = jnp.concatenate([tail[:, 0 : units - 128], tail[:, units - 128 :]], axis=0)
        hidden = jnp.concatenate([packed[0:count], rest], axis=1)
        return jnp.dot(hidden, down[r], preferred_element_type=F32)

    now = rows_step(1)
    sent = list(now)
    for copy in now:
        copy.start()
    for load in loads:
        load.wait()
    expand(0)
    for s in range(1, half + 1):
        for copy in now:
            copy.wait_recv()
        if s < half:
            now = rows_step(s + 1)
            for copy in now:
                copy.start()
            sent += now
            expand(s)
            expand(n - s)
        else:
            expand(s)

    now = hid_step(1)
    sent += now
    for copy in now:
        copy.start()

    @pl.loop(0, n)
    def _(b):
        acc[b] = shrink(0, b)

    for s in range(1, half):
        for copy in now:
            copy.wait_recv()
        now = hid_step(s + 1)
        sent += now
        for copy in now:
            copy.start()

        @pl.loop(0, n)
        def _(b):
            acc[b] += shrink(s, b) + shrink(n - s, b)

    for copy in now:
        copy.wait_recv()
    for d in (4, 3, 5, 2, 6, 1, 7, 0):
        b = lax.rem(me + d, n)
        block = (acc[b] + shrink(half, b)).astype(BF16)
        if d == 0:
            out[b] = block
        else:
            obuf[d] = block
            copy = to_peer({"ctx": b}, obuf.at[d], out.at[me], out_send.at[d], out_recv.at[n - d])
            copy.start()
            sent.append(copy)
    for d in range(1, n):
        source = lax.rem(me + d, n)
        to_peer(
            {"ctx": source}, obuf.at[d], out.at[source], out_send.at[d], out_recv.at[d]
        ).wait_recv()
    for copy in sent:
        copy.wait_send()


def run_experts(mine, down, gate_shard, up_shard):
    n = lax.axis_size("ctx")
    count, width = mine.shape
    units = gate_shard.shape[0]
    part = width // n
    packed = count + count // 2
    dma = pltpu.SemaphoreType.DMA
    anywhere = pl.BlockSpec(memory_space=pl.ANY)
    in_vmem = pl.BlockSpec(memory_space=pltpu.VMEM)
    return pl.pallas_call(
        functools.partial(moe_kernel, n),
        out_shape=jax.ShapeDtypeStruct((n, count, part), BF16),
        in_specs=[in_vmem, in_vmem, anywhere, anywhere],
        out_specs=in_vmem,
        scratch_shapes=[
            pltpu.VMEM((n, count, width), BF16),
            pltpu.VMEM((units, width), BF16),
            pltpu.VMEM((units, width), BF16),
            pltpu.VMEM((n, n, packed, 128), BF16),
            pltpu.VMEM((n, count, part), F32),
            pltpu.VMEM((n, count, part), BF16),
            dma((2,)),
        ]
        + [dma((n // 2,))] * 8
        + [dma((n,))] * 2,
        compiler_params=pltpu.CompilerParams(
            collective_id=0, has_side_effects=True, vmem_limit_bytes=48 * 2**20
        ),
        cost_estimate=pl.CostEstimate(
            flops=6 * n * count * width * units, bytes_accessed=6 * width * units, transcendentals=0
        ),
    )(mine, down, gate_shard, up_shard)


def per_device(
    hidden_in,
    queries,
    keys,
    values,
    out_weight,
    norm_gain,
    w_gate,
    w_up,
    w_down_t,
    expert_ids,
    route_gates,
):
    ctx_count = lax.axis_size("ctx")
    exp_count = lax.axis_size("exp")
    cols = exp_count // CORES
    tokens_here = hidden_in.shape[2]
    capacity = 5 * tokens_here // (4 * exp_count)
    wide = D // cols
    part = D // ctx_count
    ids = jnp.broadcast_to(expert_ids[0, 0].reshape(1, tokens_here), (exp_count, tokens_here))
    gates = jnp.broadcast_to(route_gates[0, 0], (tokens_here, 128))
    residual, mine, slots, gates_all, down = run_attend(
        queries[0, 0],
        jnp.concatenate([keys[0, 0], values[0, 0]], axis=1),
        ids,
        gates,
        norm_gain,
        hidden_in[0, 0],
        out_weight[0],
        w_down_t[0, 0].T,
        capacity,
    )
    finished = run_experts(
        mine.reshape(exp_count * capacity, D), down, w_gate[0, 0].T, w_up[0, 0].T
    )
    rows = cols * capacity
    leaving = (
        finished.reshape(cols, ctx_count // cols, CORES, rows, part)
        .transpose(0, 2, 3, 1, 4)
        .reshape(exp_count, rows, wide)
    )
    returned = lax.all_to_all(leaving, "exp", split_axis=0, concat_axis=0, tiled=True)
    selector = (
        jnp.arange(exp_count * rows, dtype=I32)[:, None] == slots[0:1]
    ).astype(BF16)
    routed = lax.dot_general(
        selector,
        returned.reshape(exp_count * rows, wide),
        (((0,), (0,)), ((), ())),
        preferred_element_type=F32,
    )
    mixture = routed * gates_all[:, :, 0].reshape(cols * tokens_here, 1)
    layer_out = (residual + mixture).astype(BF16).reshape(cols, tokens_here, wide)
    groups = [[q * CORES + c for q in range(cols)] for c in range(CORES)]
    owned = lax.all_to_all(
        layer_out, "exp", split_axis=0, concat_axis=0, tiled=True, axis_index_groups=groups
    )
    owned = owned.transpose(1, 0, 2).reshape(tokens_here, D)
    moved = passed_along(owned, "section", 1)
    return moved.reshape(1, 1, tokens_here, D)


def solution(mesh):
    return jax.shard_map(
        per_device,
        mesh=mesh,
        in_specs=(
            P("section", "exp", "ctx", None),
            P("section", "exp", "ctx", None),
            P("section", "exp", "ctx", None),
            P("section", "exp", "ctx", None),
            P("section", "ctx", None),
            P("section", None),
            P("section", "exp", None, "ctx"),
            P("section", "exp", None, "ctx"),
            P("section", "exp", None, "ctx"),
            P("section", "exp", "ctx", None),
            P("section", "exp", "ctx", None),
        ),
        out_specs=P("section", "exp", "ctx", None),
        check_vma=False,
    )
```

time: 535 us -> 364 us (0.68)
  waiting for transfers between devices: 143 us -> 39.2 us
  blocking collectives: 88.2 us -> 16.6 us
  Pallas kernels: 216 us -> 276 us
  matrix products: 32.3 us -> 2.62 us
  between operations: 13.6 us -> 0.06 us
  local copies, waits for them, and re-layouts: 23.2 us -> 10.4 us
    pallas_call x0 -> x1, Pallas kernels: none -> 108 us  [run_attend(): pl.pallas_call(functools.partial(attend_kernel, n, cols, capacity), out_s...]
    reduce_scatter x1 -> x0, waiting for transfers between devices: 106 us -> none  [per_device(): lax.psum_scatter(jnp.dot(attended, out_weight[0], preferred_element_type=...]
    all_gather x2 -> x0, blocking collectives: 59.4 us -> none  [the longest x1 39.9 us: per_device(): lax.all_gather(values[0, 0], 'ctx', axis=0, tiled=True)]
    pallas_call x1, Pallas kernels: 216 us -> 168 us  [run_experts(): pl.pallas_call(functools.partial(moe_kernel, n), out_shape=jax.ShapeDtype...]
    dot_general x5 -> x1, matrix products: 21.5 us -> 2.62 us  [per_device(): lax.dot_general(selector, returned.reshape(exp_count * rows, wide), (((0,...]
    all_to_all x1, blocking collectives: 28.7 us -> 16.6 us  [per_device(): lax.all_to_all(layer_out, 'exp', split_axis=0, concat_axis=0, tiled=True,...]
    sub x2 -> x0, matrix products: 10.7 us -> none  [attend_block(): shifted = jnp.exp(scores - jnp.max(scores, axis=-1, keepdims=True))]
    unnamed x27 -> x9, local copies, waits for them, and re-layouts: 11.6 us -> 3.69 us
  transfers between devices with their start and end apart: 4 -> 2, of which waited for: 3 -> 2; matrix products, arithmetic and copies ran while one was open for 2% -> 0% of each run, Pallas kernels for 0% -> 0%
where the time goes in v2:
time: 364 us; the launch traced here: 362 us
  Pallas kernels  276 us (76%)
  waiting for transfers between devices  39.2 us (11%)
  blocking collectives  16.6 us (5%)
  starting transfers between devices  15.3 us (4%)
  local copies, waits for them, and re-layouts  10.4 us (3%)
    pallas_call x1, Pallas kernels, run_experts(): pl.pallas_call(functools.partial(moe_kernel, n), out_shape=jax.ShapeDtype...  168 us
    pallas_call x1, Pallas kernels, run_attend(): pl.pallas_call(functools.partial(attend_kernel, n, cols, capacity), out_s...  108 us
    ppermute x1, waiting for transfers between devices, passed_along(): lax.ppermute(array, axis, [(i, (i + by) % count) for i in range(count)])  22.1 us
    all_to_all x1, waiting for transfers between devices, per_device(): lax.all_to_all(leaving, 'exp', split_axis=0, concat_axis=0, tiled=True)  17 us
    all_to_all x1, blocking collectives, per_device(): lax.all_to_all(layer_out, 'exp', split_axis=0, concat_axis=0, tiled=True,...  16.6 us
    all_to_all x1, starting transfers between devices, per_device(): lax.all_to_all(leaving, 'exp', split_axis=0, concat_axis=0, tiled=True)  13.3 us
  transfers between devices with their start and end apart: 2, of which 2 were waited for; matrix products, arithmetic and copies ran while one was open for 0% of the time, Pallas kernels for 0%

profile of v2, /device:TPU:1, one launch (start us, length us, event | category | flops | bytes accessed | tf_op | source)
XLA Modules:
  0.0 361.8 jit_solution(15053148326219529488)
XLA Ops:
  0.0 1.5 pad_maximum_fusion.kv_in
  1.5 1.2 broadcast_in_dim.16.ids_in
  2.8 1.4 broadcast_in_dim.18.gates_in
  4.1 0.0 copy-start
  4.1 108.0 %shard_map.109 = (f32[512,1024]{1,0:T(8,128)}, bf16[2,80,4096]{2,1,0:T(8,128)(2,1)}, s32[8,512]{1,0:T(8,128)}, f32[4,128,128]{2,1,0:T(8,128)}, bf16[8,192,512]{2,1,0:T(8,128)(2,1)}) custom-call(bf16[128,4096]{1,0:T(8,128)(2,1)} %bitcast.48, bf16[128,512]{1,0:T(8,128)(2,1)} %pad_maximum_fusion.kv_in, s32[8,128]{1,0:T(8,128)} %broadcast_in_dim.16.ids_in, ...), custom_call_target="tpu_custom_call" | custom-call | flops 4294967296 | bytes 8388608 | tf_op jit(solution)/shard_map/pallas_call | solution.py:410
  112.2 0.0 copy-done
  112.2 0.0 copy-start.1
  112.2 1.3 copy-done.1
  113.5 0.0 copy-start.2
  113.5 1.4 copy-done.2
  114.9 168.1 %shard_map.110 = bf16[8,160,512]{2,1,0:T(8,128)(2,1)S(1)} custom-call(bf16[160,4096]{1,0:T(8,128)(2,1)S(1)} %bitcast.32, bf16[8,192,512]{2,1,0:T(8,128)(2,1)S(1)} %copy-done.2, bf16[192,4096]{1,0:T(8,128)(2,1)S(1)} %bitcast.31, bf16[192,4096]{1,0:T(8,128)(2,1)} %bitcast.47), custom_call_target="tpu_custom_call" | custom-call | flops 6039797760 | bytes 4718592 | tf_op jit(solution)/shard_map/pallas_call | solution.py:608
  283.0 1.4 copy.17
  284.4 1.8 reshape.26
  286.1 0.0 copy-start.3
  286.2 13.3 %all-to-all-start = ((bf16[8,80,1024]{2,1,0:T(8,128)(2,1)}), bf16[8,80,1024]{2,1,0:T(8,128)(2,1)S(1)}, u32[]{:S(2)}, u32[]{:S(2)}) async-start(bf16[8,80,1024]{2,1,0:T(8,128)(2,1)} %reshape.26), calls=%async_computation | async-start | bytes 2621440 | tf_op jit(solution)/shard_map/all_to_all | solution.py:675
  299.5 0.7 slice.6
  300.2 0.0 copy-done.3
  300.2 0.1 slice_reduce_fusion
  300.3 17.0 %all-to-all-done = bf16[8,80,1024]{2,1,0:T(8,128)(2,1)S(1)} async-done(((bf16[8,80,1024]{2,1,0:T(8,128)(2,1)}), bf16[8,80,1024]{2,1,0:T(8,128)(2,1)S(1)}, u32[]{:S(2)}, u32[]{:S(2)}) %all-to-all-start) | async-done | bytes 1310752 | tf_op jit(solution)/shard_map/all_to_all | solution.py:675
  317.4 2.6 add_convert_fusion
  320.0 16.6 %all_to_all.10 = bf16[4,128,1024]{2,1,0:T(8,128)(2,1)S(1)} all-to-all(bf16[4,128,1024]{2,1,0:T(8,128)(2,1)S(1)} %bitcast.36), channel_id=1, replica_groups={{0,2,4,6},{1,3,5,7},{8,10,12,14},{9,11,13,15},{16,18,20,22},{17,19,21,2..., dimensions={0} | all-to-all | bytes 2097152 | tf_op jit(solution)/shard_map/all_to_all | solution.py:688
  336.6 0.1 copy.15
  336.7 2.0 collective-permute-start
  338.7 22.1 %collective-permute-done = bf16[128,4096]{1,0:T(8,128)(2,1)S(1)} collective-permute-done((bf16[128,4096]{1,0:T(8,128)(2,1)S(1)}, bf16[128,4096]{1,0:T(8,128)(2,1)S(1)}, u32[]{:S(2)}, u32[]{:S(2)}) %collective-permute-start) | collective-permute-done | bytes 1048608 | tf_op jit(solution)/shard_map/ppermute | solution.py:48
  360.8 1.0 copy.19
Async XLA Ops:
  4.1 108.1 %copy-start = (bf16[1,1,4096,192]{2,3,1,0:T(8,128)(2,1)S(1)}, bf16[1,1,4096,192]{2,3,1,0:T(8,128)(2,1)}, u32[]{:S(2)}) copy-start(bf16[1,1,4096,192]{2,3,1,0:T(8,128)(2,1)} %param.17) | copy-start | bytes 4718596
  112.2 1.3 copy-start.1
  113.5 1.4 copy-start.2
  286.1 14.0 %copy-start.3 = (f32[4,128,128]{2,1,0:T(8,128)S(1)}, f32[4,128,128]{2,1,0:T(8,128)}, u32[]{:S(2)}) copy-start(f32[4,128,128]{2,1,0:T(8,128)} %get-tuple-element.14) | copy-start | bytes 786436
  286.2 31.2 %all-to-all-start = ((bf16[8,80,1024]{2,1,0:T(8,128)(2,1)}), bf16[8,80,1024]{2,1,0:T(8,128)(2,1)S(1)}, u32[]{:S(2)}, u32[]{:S(2)}) async-start(bf16[8,80,1024]{2,1,0:T(8,128)(2,1)} %reshape.26), calls=%async_computation | async-start | bytes 2621440 | tf_op jit(solution)/shard_map/all_to_all | solution.py:675
  336.7 24.1 %collective-permute-start = (bf16[128,4096]{1,0:T(8,128)(2,1)S(1)}, bf16[128,4096]{1,0:T(8,128)(2,1)S(1)}, u32[]{:S(2)}, u32[]{:S(2)}) collective-permute-start(bf16[128,4096]{1,0:T(8,128)(2,1)S(1)} %bitcast.37), channel_id=1, source_target_pairs={{0,64},{64,128},{128,192},{192,0},{1,65},{65,129},{129,193},{193,1... | collective-permute-start | bytes 3145736 | tf_op jit(solution)/shard_map/ppermute | solution.py:48

commit v3 on v2

--- a/solution.py
+++ b/solution.py
@@ -41,11 +41,6 @@
 
 def across(a, b):
     return lax.dot_general(a, b, (((1,), (1,)), ((), ())), preferred_element_type=F32)
-
-
-def passed_along(array, axis, by):
-    count = lax.axis_size(axis)
-    return lax.ppermute(array, axis, [(i, (i + by) % count) for i in range(count)])
 
 
 def attend_kernel(
@@ -449,11 +444,19 @@
 
 def moe_kernel(
     n,
+    sections,
     mine,
     down,
+    residual,
+    slots,
+    gates,
     gate_any,
     up_any,
+    result,
     out,
+    back,
+    stage,
+    selector,
     rows,
     gate,
     up,
@@ -471,8 +474,21 @@
     hl_recv,
     out_send,
     out_recv,
+    back_send,
+    back_recv,
+    last_send,
+    last_recv,
 ):
     me = lax.axis_index("ctx")
+    mine_exp = lax.axis_index("exp")
+    section = lax.axis_index("section")
+    x, core = mine_exp // CORES, lax.rem(mine_exp, CORES)
+    cols, tokens = gates.shape[0], gates.shape[1]
+    experts = cols * CORES
+    per_col = n // cols
+    part = out.shape[2]
+    block_rows = back.shape[1]
+    after, before = lax.rem(section + 1, sections), lax.rem(section + sections - 1, sections)
     right, left = {"ctx": lax.rem(me + 1, n)}, {"ctx": lax.rem(me + n - 1, n)}
     half = n // 2
     count, width = mine.shape
@@ -484,7 +500,11 @@
     ]
     for load in loads:
         load.start()
-    greet([{"ctx": lax.rem(me + d, n)} for d in range(1, n)])
+    greet(
+        [{"ctx": lax.rem(me + d, n)} for d in range(1, n)]
+        + [{"exp": lax.rem(mine_exp + d, experts)} for d in range(1, experts)]
+        + [{"section": at, "exp": q * CORES + core} for at in (after, before) for q in range(cols)]
+    )
 
     def slot(r):
         return mine if r == 0 else rows.at[r]
@@ -541,6 +561,8 @@
     for load in loads:
         load.wait()
     expand(0)
+    slot_row = lax.broadcasted_iota(I32, selector.shape, 0)
+    selector[...] = jnp.where(slot_row == slots[0:1], 1.0, 0.0).astype(BF16)
     for s in range(1, half + 1):
         for copy in now:
             copy.wait_recv()
@@ -577,40 +599,121 @@
 
     for copy in now:
         copy.wait_recv()
-    for d in (4, 3, 5, 2, 6, 1, 7, 0):
+
+    def finish(d):
         b = lax.rem(me + d, n)
         block = (acc[b] + shrink(half, b)).astype(BF16)
         if d == 0:
-            out[b] = block
+            out[me] = block
         else:
             obuf[d] = block
             copy = to_peer({"ctx": b}, obuf.at[d], out.at[me], out_send.at[d], out_recv.at[n - d])
             copy.start()
             sent.append(copy)
-    for d in range(1, n):
-        source = lax.rem(me + d, n)
-        to_peer(
-            {"ctx": source}, obuf.at[d], out.at[source], out_send.at[d], out_recv.at[d]
-        ).wait_recv()
+
+    def hand_back(r, c):
+        source = lax.rem(me + r, n)
+        owner = source // per_col * CORES + c
+        side = lax.rem(source, per_col)
+        rel = lax.rem(mine_exp - owner + experts, experts)
+        src = out.at[source, pl.ds(c * block_rows, block_rows)]
+        dst = back.at[mine_exp, :, lanes(side * part, part)]
+        there = to_peer({"exp": owner}, src, dst, back_send.at[r, c], back_recv.at[rel, side])
+        return owner, there, (src, dst, back_recv.at[0, side])
+
+    def forward(r):
+        if r > 0:
+            source = lax.rem(me + r, n)
+            to_peer(
+                {"ctx": source}, obuf.at[r], out.at[source], out_send.at[r], out_recv.at[r]
+            ).wait_recv()
+        for c in range(CORES):
+            owner, there, here = hand_back(r, c)
+
+            @pl.when(owner != mine_exp)
+            def _():
+                there.start()
+
+            @pl.when(owner == mine_exp)
+            def _():
+                pltpu.make_async_copy(*here).start()
+
+    for d in (4, 3, 5):
+        finish(d)
+    finish(0)
+    forward(0)
+    for d in (2, 6, 1, 7):
+        finish(d)
+    for r in (7, 1, 6, 2, 5, 3, 4):
+        forward(r)
+
+    def last(side, q, source):
+        dst = result.at[:, lanes(source * (per_col * part) + side * part, part)]
+        return to_peer(
+            {"section": after, "exp": q * CORES + core},
+            stage.at[side, q],
+            dst,
+            last_send.at[side, q],
+            last_recv.at[side, source],
+        )
+
+    gate_column = gates[...].reshape(cols * tokens, 128)[:, 0:1]
+    for side in range(per_col):
+        for e in range(experts):
+            rel = lax.rem(e - mine_exp + experts, experts)
+            landed = back.at[e, :, pl.ds(side * part, part)]
+            pltpu.make_async_copy(landed, landed, back_recv.at[rel, side]).wait()
+        routed = lax.dot_general(
+            selector[...],
+            back[:, :, side * part : (side + 1) * part].reshape(experts * block_rows, part),
+            (((0,), (0,)), ((), ())),
+            preferred_element_type=F32,
+        )
+        mixture = routed * gate_column + residual[:, side * part : (side + 1) * part]
+        stage[side] = mixture.astype(BF16).reshape(cols, tokens, part)
+        for q in range(cols):
+            last(side, q, x).start()
+    for side in range(per_col):
+        for q in range(cols):
+            last(side, q, q).wait_recv()
+    for side in range(per_col):
+        for q in range(cols):
+            last(side, q, x).wait_send()
+    for r in range(n):
+        for c in range(CORES):
+            owner, there, _ = hand_back(r, c)
+
+            @pl.when(owner != mine_exp)
+            def _():
+                there.wait_send()
+
     for copy in sent:
         copy.wait_send()
 
 
-def run_experts(mine, down, gate_shard, up_shard):
+def run_experts(mine, down, residual, slots, gates, gate_shard, up_shard):
     n = lax.axis_size("ctx")
+    sections = lax.axis_size("section")
+    cols, tokens = gates.shape[0], gates.shape[1]
+    experts = cols * CORES
     count, width = mine.shape
     units = gate_shard.shape[0]
     part = width // n
+    wide = width // cols
     packed = count + count // 2
     dma = pltpu.SemaphoreType.DMA
     anywhere = pl.BlockSpec(memory_space=pl.ANY)
     in_vmem = pl.BlockSpec(memory_space=pltpu.VMEM)
     return pl.pallas_call(
-        functools.partial(moe_kernel, n),
-        out_shape=jax.ShapeDtypeStruct((n, count, part), BF16),
-        in_specs=[in_vmem, in_vmem, anywhere, anywhere],
+        functools.partial(moe_kernel, n, sections),
+        out_shape=jax.ShapeDtypeStruct((tokens, width), BF16),
+        in_specs=[in_vmem] * 5 + [anywhere] * 2,
         out_specs=in_vmem,
         scratch_shapes=[
+            pltpu.VMEM((n, count, part), BF16),
+            pltpu.VMEM((experts, count // CORES, wide), BF16),
+            pltpu.VMEM((wide // part, cols, tokens, part), BF16),
+            pltpu.VMEM((experts * count // CORES, cols * tokens), BF16),
             pltpu.VMEM((n, count, width), BF16),
             pltpu.VMEM((units, width), BF16),
             pltpu.VMEM((units, width), BF16),
@@ -620,14 +723,16 @@
             dma((2,)),
         ]
         + [dma((n // 2,))] * 8
-        + [dma((n,))] * 2,
+        + [dma((n,))] * 2
+        + [dma((n, CORES)), dma((experts, wide // part))]
+        + [dma((wide // part, cols))] * 2,
         compiler_params=pltpu.CompilerParams(
-            collective_id=0, has_side_effects=True, vmem_limit_bytes=48 * 2**20
+            collective_id=0, has_side_effects=True, vmem_limit_bytes=56 * 2**20
         ),
         cost_estimate=pl.CostEstimate(
             flops=6 * n * count * width * units, bytes_accessed=6 * width * units, transcendentals=0
         ),
-    )(mine, down, gate_shard, up_shard)
+    )(mine, down, residual, slots, gates, gate_shard, up_shard)
 
 
 def per_device(
@@ -643,13 +748,9 @@
     expert_ids,
     route_gates,
 ):
-    ctx_count = lax.axis_size("ctx")
     exp_count = lax.axis_size("exp")
-    cols = exp_count // CORES
     tokens_here = hidden_in.shape[2]
     capacity = 5 * tokens_here // (4 * exp_count)
-    wide = D // cols
-    part = D // ctx_count
     ids = jnp.broadcast_to(expert_ids[0, 0].reshape(1, tokens_here), (exp_count, tokens_here))
     gates = jnp.broadcast_to(route_gates[0, 0], (tokens_here, 128))
     residual, mine, slots, gates_all, down = run_attend(
@@ -663,33 +764,15 @@
         w_down_t[0, 0].T,
         capacity,
     )
-    finished = run_experts(
-        mine.reshape(exp_count * capacity, D), down, w_gate[0, 0].T, w_up[0, 0].T
-    )
-    rows = cols * capacity
-    leaving = (
-        finished.reshape(cols, ctx_count // cols, CORES, rows, part)
-        .transpose(0, 2, 3, 1, 4)
-        .reshape(exp_count, rows, wide)
-    )
-    returned = lax.all_to_all(leaving, "exp", split_axis=0, concat_axis=0, tiled=True)
-    selector = (
-        jnp.arange(exp_count * rows, dtype=I32)[:, None] == slots[0:1]
-    ).astype(BF16)
-    routed = lax.dot_general(
-        selector,
-        returned.reshape(exp_count * rows, wide),
-        (((0,), (0,)), ((), ())),
-        preferred_element_type=F32,
-    )
-    mixture = routed * gates_all[:, :, 0].reshape(cols * tokens_here, 1)
-    layer_out = (residual + mixture).astype(BF16).reshape(cols, tokens_here, wide)
-    groups = [[q * CORES + c for q in range(cols)] for c in range(CORES)]
-    owned = lax.all_to_all(
-        layer_out, "exp", split_axis=0, concat_axis=0, tiled=True, axis_index_groups=groups
-    )
-    owned = owned.transpose(1, 0, 2).reshape(tokens_here, D)
-    moved = passed_along(owned, "section", 1)
+    moved = run_experts(
+        mine.reshape(exp_count * capacity, D),
+        down,
+        residual,
+        slots,
+        gates_all,
+        w_gate[0, 0].T,
+        w_up[0, 0].T,
+    )
     return moved.reshape(1, 1, tokens_here, D)
 
 

time: 364 us -> 330 us (0.907)
  Pallas kernels: 276 us -> 321 us
  waiting for transfers between devices: 39.2 us -> 0 us
  blocking collectives: 16.6 us -> 0 us
  starting transfers between devices: 15.3 us -> 0 us
  local copies, waits for them, and re-layouts: 10.4 us -> 4.9 us
    pallas_call x1, Pallas kernels: 168 us -> 213 us  [run_experts(): pl.pallas_call(functools.partial(moe_kernel, n, sections), out_shape=jax....]
    ppermute x1 -> x0, waiting for transfers between devices: 22.1 us -> none  [passed_along(): lax.ppermute(array, axis, [(i, (i + by) % count) for i in range(count)])]
    all_to_all x1 -> x0, waiting for transfers between devices: 17 us -> none  [per_device(): lax.all_to_all(leaving, 'exp', split_axis=0, concat_axis=0, tiled=True)]
    all_to_all x1 -> x0, blocking collectives: 16.6 us -> none  [per_device(): lax.all_to_all(layer_out, 'exp', split_axis=0, concat_axis=0, tiled=True,...]
    all_to_all x1 -> x0, starting transfers between devices: 13.3 us -> none  [per_device(): lax.all_to_all(leaving, 'exp', split_axis=0, concat_axis=0, tiled=True)]
  transfers between devices with their start and end apart: 2 -> 0, of which waited for: 2 -> 0; matrix products, arithmetic and copies ran while one was open for 0% -> 0% of each run, Pallas kernels for 0% -> 0%
where the time goes in v3:
time: 330 us; the launch traced here: 328 us
  Pallas kernels  321 us (97%)
  local copies, waits for them, and re-layouts  4.9 us (1%)
    pallas_call x1, Pallas kernels, run_experts(): pl.pallas_call(functools.partial(moe_kernel, n, sections), out_shape=jax....  213 us
    pallas_call x1, Pallas kernels, run_attend(): pl.pallas_call(functools.partial(attend_kernel, n, cols, capacity), out_s...  108 us

profile of v3, /device:TPU:1, one launch (start us, length us, event | category | flops | bytes accessed | tf_op | source)
XLA Modules:
  0.0 327.7 jit_solution(10461112855068361841)
XLA Ops:
  0.0 1.2 broadcast_in_dim.15.ids_in
  1.2 1.4 broadcast_in_dim.17.gates_in
  2.6 1.5 pad_maximum_fusion.kv_in
  4.1 108.1 %shard_map.109 = (f32[512,1024]{1,0:T(8,128)}, bf16[2,80,4096]{2,1,0:T(8,128)(2,1)}, s32[8,512]{1,0:T(8,128)}, f32[4,128,128]{2,1,0:T(8,128)}, bf16[8,192,512]{2,1,0:T(8,128)(2,1)}) custom-call(bf16[128,4096]{1,0:T(8,128)(2,1)} %bitcast.27, bf16[128,512]{1,0:T(8,128)(2,1)} %pad_maximum_fusion.kv_in, s32[8,128]{1,0:T(8,128)} %broadcast_in_dim.15.ids_in, ...), custom_call_target="tpu_custom_call" | custom-call | flops 4294967296 | bytes 8388608 | tf_op jit(solution)/shard_map/pallas_call | solution.py:405
  112.3 213.2 %shard_map.110 = bf16[128,4096]{1,0:T(8,128)(2,1)} custom-call(bf16[160,4096]{1,0:T(8,128)(2,1)} %bitcast.29, bf16[8,192,512]{2,1,0:T(8,128)(2,1)} %get-tuple-element.11.down, f32[512,1024]{1,0:T(8,128)} %get-tuple-element.12.residual, s32[8,512]{1,0:T(8,128)} %get-tuple-element.13.slots, f32[4,128,128]{2,1,0:T(8,128)} %get-tuple-element.14.gates, ...), custom_call_target="tpu_custom_call" | custom-call | flops 6039797760 | bytes 4718592 | tf_op jit(solution)/shard_map/pallas_call | solution.py:707
  325.4 2.3 copy.13

commit v4 on v2

v4 whole, which is shorter than its diff:
```python
import functools
import math

import jax
import jax.numpy as jnp
from jax import lax
from jax.experimental import pallas as pl
from jax.experimental.pallas import tpu as pltpu
from jax.sharding import PartitionSpec as P

D = 4096
QUERY_HEADS = 32
KEY_VALUE_HEADS = 2
HEAD_SIZE = 128
CORES = 2
MESH = pl.DeviceIdType.MESH
BF16, F32, I32 = jnp.bfloat16, jnp.float32, jnp.int32


def to_peer(peer, src, dst, send_sem, recv_sem):
    return pltpu.make_async_remote_copy(
        src_ref=src,
        dst_ref=dst,
        send_sem=send_sem,
        recv_sem=recv_sem,
        device_id=peer,
        device_id_type=MESH,
    )


def greet(peers):
    barrier = pltpu.get_barrier_semaphore()
    for peer in peers:
        pl.semaphore_signal(barrier, inc=1, device_id=peer, device_id_type=MESH)
    pl.semaphore_wait(barrier, len(peers))


def lanes(start, size):
    return pl.ds(pl.multiple_of(start, 128), size)


def across(a, b):
    return lax.dot_general(a, b, (((1,), (1,)), ((), ())), preferred_element_type=F32)


def layer_kernel(
    n,
    cols,
    sections,
    capacity,
    query,
    key_in,
    value_in,
    ids_in,
    gates_in,
    gain,
    hidden_any,
    weight_any,
    gate_any,
    up_any,
    down_any,
    result,
    kv,
    mixed,
    weight,
    hidden,
    ids,
    gates,
    squares,
    bias,
    residual,
    selector,
    selector_t,
    outgoing,
    rows,
    gate,
    up,
    down,
    hid,
    acc,
    obuf,
    out,
    back,
    stage,
    local_sem,
    gate_sem,
    up_sem,
    kr_send,
    kr_recv,
    kl_send,
    kl_recv,
    wr_send,
    wr_recv,
    wl_send,
    wl_recv,
    sib_send,
    sib_recv,
    x_send,
    x_recv,
    small_send,
    small_recv,
    sq_send,
    sq_recv,
    wd_send,
    wd_recv,
    disp_send,
    disp_recv,
    rr_send,
    rr_recv,
    rl_send,
    rl_recv,
    hr_send,
    hr_recv,
    hl_send,
    hl_recv,
    out_send,
    out_recv,
    back_send,
    back_recv,
    last_send,
    last_recv,
):
    z = lax.axis_index("ctx")
    me = lax.axis_index("exp")
    section = lax.axis_index("section")
    x, core = me // CORES, lax.rem(me, CORES)
    experts = cols * CORES
    half = n // 2
    tokens, width = query.shape
    wide = width // cols
    chunk = width // n
    part = width // n
    per_col = n // cols
    heads = chunk // HEAD_SIZE
    group = QUERY_HEADS // KEY_VALUE_HEADS // heads
    streams = rows.shape[1]
    stream = wide // streams
    count = rows.shape[2]
    block_rows = count // CORES
    units = gate.shape[1]
    pair = count // 2
    piece = 128
    pieces = part // piece
    up_z, down_z = {"ctx": lax.rem(z + 1, n)}, {"ctx": lax.rem(z + n - 1, n)}
    col = [lax.rem(x + d, cols) for d in range(cols)]
    same = [{"exp": col[d] * CORES + core} for d in range(cols)]
    sibling = {"exp": x * CORES + 1 - core}
    after, before = lax.rem(section + 1, sections), lax.rem(section + sections - 1, sections)

    loads = [
        pltpu.make_async_copy(
            weight_any.at[:, lanes(x * wide, chunk)], weight.at[z, 0], local_sem.at[0]
        ),
        pltpu.make_async_copy(
            weight_any.at[:, lanes(x * wide + chunk, chunk)], weight.at[z, 1], local_sem.at[1]
        ),
        pltpu.make_async_copy(hidden_any.at[:, lanes(x * wide, wide)], hidden.at[x], local_sem.at[2]),
        pltpu.make_async_copy(down_any.at[:, lanes(z * part, part)], down.at[0], local_sem.at[3]),
    ]
    expert_loads = [
        pltpu.make_async_copy(
            src.at[:, pl.ds(q * wide + h * stream, stream)],
            dst.at[h, :, pl.ds(q * stream, stream)],
            sem.at[h, q],
        )
        for src, dst, sem in ((gate_any, gate, gate_sem), (up_any, up, up_sem))
        for h in range(streams)
        for q in range(cols)
    ]
    for copy in loads + expert_loads:
        copy.start()
    kv[z, :, 0 : key_in.shape[1]] = key_in[...]
    kv[z, :, key_in.shape[1] :] = value_in[...]
    ids[x] = jnp.broadcast_to(ids_in[...], ids.shape[1:])
    gates[x] = jnp.transpose(jnp.broadcast_to(gates_in[...], (128, tokens)))
    greet(
        [{"ctx": lax.rem(z + d, n)} for d in range(1, n)]
        + [{"exp": lax.rem(me + d, experts)} for d in range(1, experts)]
        + [{"section": at, "exp": q * CORES + core} for at in (after, before) for q in range(cols)]
    )

    def kv_step(s):
        a, b = lax.rem(z + n + 1 - s, n), lax.rem(z + s - 1, n)
        cut = tokens // 2
        one, two = kv.at[a], kv.at[b]
        if s == half:
            one, two = kv.at[a, pl.ds(0, cut)], kv.at[b, pl.ds(cut, cut)]
        return (
            to_peer(up_z, one, one, kr_send.at[s - 1], kr_recv.at[s - 1]),
            to_peer(down_z, two, two, kl_send.at[s - 1], kl_recv.at[s - 1]),
        )

    def weight_step(s):
        a, b = lax.rem(z + n + 1 - s, n), lax.rem(z + s - 1, n)
        cut = chunk // 2
        one, two = weight.at[a, core], weight.at[b, core]
        if s == half:
            one, two = weight.at[a, core, pl.ds(0, cut)], weight.at[b, core, pl.ds(cut, cut)]
        own = weight_any.at[:, lanes(x * wide + core * chunk, chunk)]
        return (
            to_peer(up_z, own if s == 1 else one, one, wr_send.at[s - 1], wr_recv.at[s - 1]),
            to_peer(down_z, own if s == 1 else two, two, wl_send.at[s - 1], wl_recv.at[s - 1]),
        )

    def share(off):
        k = lax.rem(z + off, n)
        return to_peer(
            sibling, weight.at[k, core], weight.at[k, core], sib_send.at[off], sib_recv.at[off]
        )

    def shared(off):
        k = lax.rem(z + off, n)
        return to_peer(
            sibling, weight.at[k, 1 - core], weight.at[k, 1 - core], sib_send.at[off], sib_recv.at[off]
        )

    def weight_arrived(s):
        for copy in weight_step(s):
            copy.wait_recv()
        if s < half:
            for copy in weight_step(s + 1):
                copy.start()
            share(n - s).start()
        share(s).start()

    small = []
    for d in range(1, cols):
        for at, (src, dst) in enumerate(
            (
                (ids.at[x], ids.at[x]),
                (gates.at[x], gates.at[x]),
                (hidden_any.at[:, lanes(col[d] * wide, wide)], hidden.at[x]),
            )
        ):
            small.append(
                to_peer(same[d], src, dst, small_send.at[d, at], small_recv.at[cols - d, at])
            )
    now = kv_step(1)
    for copy in now:
        copy.start()
    for copy in small:
        copy.start()

    row = lax.broadcasted_iota(I32, (tokens, n * tokens), 0) + z * tokens
    column = lax.broadcasted_iota(I32, (tokens, n * tokens), 1)
    bias[...] = jnp.where(row >= column, 0.0, -1e30)
    residual[...] = jnp.zeros_like(residual)

    for s in range(1, half + 1):
        for copy in now:
            copy.wait_recv()
        if s < half:
            now = kv_step(s + 1)
            for copy in now:
                copy.start()
    for copy in weight_step(1):
        copy.start()

    def place(j):
        odd = lax.rem(j, 2)
        off = odd * ((j + 1) // 2) + (1 - odd) * lax.rem(n - j // 2, n)
        return off, lax.rem(z + off, n)

    def chunk_first(j):
        _, k = place(j)
        return (
            to_peer(same[1], mixed.at[k, x], mixed.at[k, x], x_send.at[j, 0], x_recv.at[j, 0]),
            to_peer(same[cols - 1], mixed.at[k, x], mixed.at[k, x], x_send.at[j, 1], x_recv.at[j, 1]),
        )

    def chunk_second(j):
        _, k = place(j)
        cut = tokens // 2
        one = mixed.at[k, col[cols - 1], pl.ds(0, cut)]
        two = mixed.at[k, col[1], pl.ds(cut, cut)]
        return (
            to_peer(same[1], one, one, x_send.at[j, 2], x_recv.at[j, 2]),
            to_peer(same[cols - 1], two, two, x_send.at[j, 3], x_recv.at[j, 3]),
        )

    def chunk_forward(j):
        for copy in chunk_first(j):
            copy.wait_recv()
        for copy in chunk_second(j):
            copy.start()

    def project(j):
        off, k = place(j)
        for copy in chunk_second(j):
            copy.wait_recv()

        @pl.when(off > 0)
        def _():
            shared(off).wait_recv()

        left = mixed[k].reshape(cols * tokens, chunk)
        for side in range(CORES):
            residual[:, side * chunk : (side + 1) * chunk] += jnp.dot(
                left, weight[k, side], preferred_element_type=F32
            )

    scale = math.log2(math.e) / math.sqrt(HEAD_SIZE)

    @pl.loop(0, n)
    def _(j):
        _, k = place(j)
        kv_head = k // group
        key = kv[:, :, lanes(kv_head * HEAD_SIZE, HEAD_SIZE)].reshape(n * tokens, HEAD_SIZE)
        value = kv[
            :, :, lanes((KEY_VALUE_HEADS + kv_head) * HEAD_SIZE, HEAD_SIZE)
        ].reshape(n * tokens, HEAD_SIZE)
        for h in range(heads):
            scores = across(query[:, lanes(k * chunk + h * HEAD_SIZE, HEAD_SIZE)], key) + bias[...]
            top = jnp.max(scores, axis=-1, keepdims=True)
            shifted = jnp.exp2((scores - top) * scale)
            total = jnp.sum(shifted, axis=-1, keepdims=True)
            attended = jnp.dot(shifted.astype(BF16), value, preferred_element_type=F32)
            mixed[k, x, :, h * HEAD_SIZE : (h + 1) * HEAD_SIZE] = (attended / total).astype(BF16)
        for copy in chunk_first(j):
            copy.start()

        @pl.when(j >= 1)
        def _():
            chunk_forward(j - 1)

        @pl.when(j == 2)
        def _():
            loads[0].wait()
            loads[1].wait()
            weight_arrived(1)

        @pl.when(j == 5)
        def _():
            weight_arrived(2)

        @pl.when(j >= 3)
        def _():
            project(j - 3)

    chunk_forward(n - 1)
    weight_arrived(3)
    project(n - 3)
    project(n - 2)
    weight_arrived(4)
    downs = []
    for d in (4, 3, 5, 2, 6, 1, 7):
        peer = lax.rem(z + d, n)
        downs.append(
            to_peer(
                {"ctx": peer},
                down_any.at[:, lanes(peer * part, part)],
                down.at[n - d],
                wd_send.at[d],
                wd_recv.at[n - d],
            )
        )
        downs[-1].start()
    for copy in small:
        copy.wait_recv()
    loads[2].wait()

    expert = lax.broadcasted_iota(I32, (experts, tokens), 0)
    earlier = lax.broadcasted_iota(I32, (tokens, tokens), 0) < lax.broadcasted_iota(
        I32, (tokens, tokens), 1
    )
    earlier = jnp.where(earlier, 1.0, 0.0).astype(BF16)
    placed = []
    for q in range(cols):
        chosen = ids[q]
        named = jnp.where(expert == chosen, 1.0, 0.0)
        ahead = jnp.dot(named.astype(BF16), earlier, preferred_element_type=F32)
        rank = jnp.sum(ahead * named, axis=0, keepdims=True)
        placed.append(
            (chosen[0:1] * (cols * capacity) + q * capacity).astype(F32) + rank
        )
    placed = jnp.concatenate(placed, axis=1)
    slot = lax.broadcasted_iota(I32, selector.shape, 0).astype(F32)
    selector[...] = jnp.where(slot == placed, 1.0, 0.0).astype(BF16)
    placed_t = jnp.transpose(jnp.broadcast_to(placed, (8, cols * tokens)))[:, 0:1]
    slot = lax.broadcasted_iota(I32, selector_t.shape, 1).astype(F32)
    selector_t[...] = jnp.where(slot == placed_t, 1.0, 0.0).astype(BF16)

    project(n - 1)
    residual[...] += hidden[...].reshape(cols * tokens, wide).astype(F32)
    res = residual[...]
    squares[x] = lax.dot_general(
        jnp.ones((8, wide), F32),
        res * res,
        (((1,), (1,)), ((), ())),
        precision=lax.Precision.HIGHEST,
        preferred_element_type=F32,
    )
    sums = [
        to_peer(same[d], squares.at[x], squares.at[x], sq_send.at[d], sq_recv.at[cols - d])
        for d in range(1, cols)
    ]
    for copy in sums:
        copy.start()
    for copy in sums:
        copy.wait_recv()
    total = squares[0]
    for q in range(1, cols):
        total += squares[q]
    inverse = jnp.transpose(lax.rsqrt(total * (1.0 / width) + 1e-06))[:, 0:1]

    def rows_place(h):
        return rows.at[0, h, pl.ds(pl.multiple_of(core * block_rows, 16), block_rows), lanes(x * stream, stream)]

    def dispatch(h):
        columns = residual[:, h * stream : (h + 1) * stream]
        gains = gain[:, lanes(x * wide + h * stream, stream)].astype(F32)
        normed = (columns * inverse * gains).astype(BF16)
        picked = jnp.dot(selector[...], normed, preferred_element_type=F32).astype(BF16)
        outgoing[h] = picked.reshape(experts, block_rows, stream)
        copies = []
        for d in (4, 5, 2, 6, 3, 7, 1):
            e = lax.rem(me + d, experts)
            copies.append(
                to_peer(
                    {"exp": e},
                    outgoing.at[h, e],
                    rows_place(h),
                    disp_send.at[d, h],
                    disp_recv.at[experts - d, h],
                )
            )
            copies[-1].start()
        keep = pltpu.make_async_copy(outgoing.at[h, me], rows_place(h), disp_recv.at[0, h])
        keep.start()
        return copies, keep

    def rows_step(s, h):
        copies = []
        if s < half or h % 2 == 0:
            src, dst = rows.at[(n + 1 - s) % n, h], rows.at[n - s, h]
            copies.append(to_peer(up_z, src, dst, rr_send.at[s - 1, h], rr_recv.at[s - 1, h]))
        if s < half or h % 2 == 1:
            src, dst = rows.at[s - 1, h], rows.at[s, h]
            copies.append(to_peer(down_z, src, dst, rl_send.at[s - 1, h], rl_recv.at[s - 1, h]))
        return copies

    def expand(r):
        gate_part, up_part = 0.0, 0.0
        for h in range(streams):
            block = rows[r, h]
            gate_part += across(block, gate[h])
            up_part += across(block, up[h])
        shown = (gate_part / (1.0 + jnp.exp(-gate_part)) * up_part).astype(BF16)
        owner = lax.rem(z + r, n)
        hid[0, owner, 0:count, :] = shown[:, 0:128]
        hid[0, owner, count : count + pair, :] = jnp.concatenate(
            [shown[0:pair, 128:units], shown[pair:count, 128:units]], axis=1
        )

    dispatched = [dispatch(h) for h in range(streams)]
    sent = []
    steps = {}
    for h in range(streams):
        copies, keep = dispatched[h]
        sent += copies
        for copy in copies:
            copy.wait_recv()
        keep.wait()
        steps[1, h] = rows_step(1, h)
        for copy in steps[1, h]:
            copy.start()
    for copy in expert_loads:
        copy.wait()
    expand(0)
    for s in range(1, half + 1):
        for h in range(streams):
            for copy in steps[s, h]:
                copy.wait_recv()
            if s < half:
                steps[s + 1, h] = rows_step(s + 1, h)
                for copy in steps[s + 1, h]:
                    copy.start()
        expand(s)
        if s < half:
            expand(n - s)
    for copies in steps.values():
        sent += copies

    def hid_step(s):
        one, two = hid.at[(n + 1 - s) % n], hid.at[s - 1]
        here, there = hid.at[n - s], hid.at[s]
        if s == half:
            one, here = one.at[pl.ds(0, half)], here.at[pl.ds(0, half)]
            two, there = two.at[pl.ds(half, half)], there.at[pl.ds(half, half)]
        return (
            to_peer(up_z, one, here, hr_send.at[s - 1], hr_recv.at[s - 1]),
            to_peer(down_z, two, there, hl_send.at[s - 1], hl_recv.at[s - 1]),
        )

    def unpack(r, b):
        packed = hid[r, b]
        end = packed[count : count + pair]
        rest = jnp.concatenate([end[:, 0 : units - 128], end[:, units - 128 :]], axis=0)
        return jnp.concatenate([packed[0:count], rest], axis=1)

    def shrink(r, b):
        return jnp.dot(unpack(r, b), down[r], preferred_element_type=F32)

    now = hid_step(1)
    sent += now
    for copy in now:
        copy.start()
    loads[3].wait()
    for copy in downs:
        copy.wait_recv()

    @pl.loop(0, n)
    def _(b):
        acc[b] = shrink(0, b)

    for s in range(1, half):
        for copy in now:
            copy.wait_recv()
        now = hid_step(s + 1)
        sent += now
        for copy in now:
            copy.start()

        @pl.loop(0, n)
        def _(b):
            acc[b] += shrink(s, b) + shrink(n - s, b)

    for copy in now:
        copy.wait_recv()

    def leave(d, i):
        b = lax.rem(z + d, n)
        window = lanes(i * piece, piece)
        return to_peer(
            {"ctx": b},
            obuf.at[d, :, window],
            out.at[z, :, window],
            out_send.at[d, i],
            out_recv.at[n - d, i],
        )

    def finish(i):
        window = lanes(i * piece, piece)
        for d in (4, 3, 5, 2, 6, 1, 7, 0):
            b = lax.rem(z + d, n)
            block = acc[b, :, window] + jnp.dot(
                unpack(half, b), down[half, :, window], preferred_element_type=F32
            )
            if d == 0:
                out[z, :, window] = block.astype(BF16)
            else:
                obuf[d, :, window] = block.astype(BF16)
                leave(d, i).start()

    def hand_back(r, c, i):
        source = lax.rem(z + r, n)
        owner = source // per_col * CORES + c
        side = lax.rem(source, per_col)
        rel = lax.rem(me - owner + experts, experts)
        src = out.at[source, pl.ds(c * block_rows, block_rows), lanes(i * piece, piece)]
        dst = back.at[me, :, lanes(side * part + i * piece, piece)]
        there = to_peer({"exp": owner}, src, dst, back_send.at[r, c, i], back_recv.at[rel, side, i])
        return owner, there, (src, dst, back_recv.at[0, side, i])

    def forward(i):
        for r in (0, 7, 1, 6, 2, 5, 3, 4):
            if r > 0:
                source = lax.rem(z + r, n)
                landed = out.at[source, :, lanes(i * piece, piece)]
                pltpu.make_async_copy(landed, landed, out_recv.at[r, i]).wait()
            for c in range(CORES):
                owner, there, here = hand_back(r, c, i)

                @pl.when(owner != me)
                def _():
                    there.start()

                @pl.when(owner == me)
                def _():
                    pltpu.make_async_copy(*here).start()

    def last(side, q, source, i):
        dst = result.at[:, lanes(source * wide + side * part + i * piece, piece)]
        return to_peer(
            {"section": after, "exp": q * CORES + core},
            stage.at[i, side, q],
            dst,
            last_send.at[i, side, q],
            last_recv.at[i, side, source],
        )

    gate_column = gates[...].reshape(cols * tokens, 128)[:, 0:1]

    def combine(i):
        for side in range(per_col):
            window = lanes(side * part + i * piece, piece)
            for e in range(experts):
                rel = lax.rem(e - me + experts, experts)
                landed = back.at[e, :, window]
                pltpu.make_async_copy(landed, landed, back_recv.at[rel, side, i]).wait()
            routed = jnp.dot(
                selector_t[...],
                back[:, :, window].reshape(experts * block_rows, piece),
                preferred_element_type=F32,
            )
            mixture = routed * gate_column + residual[:, window]
            stage[i, side] = mixture.astype(BF16).reshape(cols, tokens, piece)
            for q in range(cols):
                last(side, q, x, i).start()

    @pl.loop(0, pieces + 2)
    def _(t):
        @pl.when(t < pieces)
        def _():
            finish(t)

        @pl.when((t >= 1) & (t < pieces + 1))
        def _():
            forward(t - 1)

        @pl.when(t >= 2)
        def _():
            combine(t - 2)

    @pl.loop(0, pieces)
    def _(i):
        for side in range(per_col):
            for q in range(cols):
                last(side, q, q, i).wait_recv()
                last(side, q, x, i).wait_send()
        for r in range(n):
            if r > 0:
                leave(r, i).wait_send()
            for c in range(CORES):
                owner, there, _ = hand_back(r, c, i)

                @pl.when(owner != me)
                def _():
                    there.wait_send()

    for copy in small + sums + sent + downs:
        copy.wait_send()
    for s in range(1, half + 1):
        for copy in kv_step(s) + weight_step(s):
            copy.wait_send()
    for off in range(1, n):
        share(off).wait_send()

    @pl.loop(0, n)
    def _(j):
        for copy in chunk_first(j) + chunk_second(j):
            copy.wait_send()


def run_layer(query, key, value, ids, gates, gain, hidden, weight, gate, up, down):
    n = lax.axis_size("ctx")
    experts = lax.axis_size("exp")
    sections = lax.axis_size("section")
    cols = experts // CORES
    tokens, width = query.shape
    wide, part = width // cols, width // n
    units = down.shape[0]
    capacity = 5 * tokens // (4 * experts)
    count = experts * capacity
    packed = count + count // 2
    streams = 2
    pieces = part // 128
    dma = pltpu.SemaphoreType.DMA
    anywhere = pl.BlockSpec(memory_space=pl.ANY)
    in_vmem = pl.BlockSpec(memory_space=pltpu.VMEM)
    ring = [dma((n // 2,))] * 4
    return pl.pallas_call(
        functools.partial(layer_kernel, n, cols, sections, capacity),
        out_shape=jax.ShapeDtypeStruct((tokens, width), BF16),
        in_specs=[in_vmem] * 6 + [anywhere] * 5,
        out_specs=in_vmem,
        scratch_shapes=[
            pltpu.VMEM((n, tokens, 2 * key.shape[1]), BF16),
            pltpu.VMEM((n, cols, tokens, part), BF16),
            pltpu.VMEM((n, CORES, part, part), BF16),
            pltpu.VMEM((cols, tokens, wide), BF16),
            pltpu.VMEM((cols, experts, tokens), I32),
            pltpu.VMEM((cols, tokens, 128), F32),
            pltpu.VMEM((cols, 8, cols * tokens), F32),
            pltpu.VMEM((tokens, n * tokens), F32),
            pltpu.VMEM((cols * tokens, wide), F32),
            pltpu.VMEM((experts * cols * capacity, cols * tokens), BF16),
            pltpu.VMEM((cols * tokens, experts * cols * capacity), BF16),
            pltpu.VMEM((streams, experts, count // CORES, wide // streams), BF16),
            pltpu.VMEM((n, streams, count, width // streams), BF16),
            pltpu.VMEM((streams, units, width // streams), BF16),
            pltpu.VMEM((streams, units, width // streams), BF16),
            pltpu.VMEM((n, units, part), BF16),
            pltpu.VMEM((n, n, packed, 128), BF16),
            pltpu.VMEM((n, count, part), F32),
            pltpu.VMEM((n, count, part), BF16),
            pltpu.VMEM((n, count, part), BF16),
            pltpu.VMEM((experts, count // CORES, wide), BF16),
            pltpu.VMEM((pieces, wide // part, cols, tokens, 128), BF16),
            dma((4,)),
            dma((streams, cols)),
            dma((streams, cols)),
        ]
        + ring
        + ring
        + [dma((n,))] * 2
        + [dma((n, 4))] * 2
        + [dma((cols, 3))] * 2
        + [dma((cols,))] * 2
        + [dma((n,))] * 2
        + [dma((experts, streams))] * 2
        + [dma((n // 2, streams))] * 4
        + ring
        + [dma((n, pieces))] * 2
        + [dma((n, CORES, pieces)), dma((experts, wide // part, pieces))]
        + [dma((pieces, wide // part, cols))] * 2,
        compiler_params=pltpu.CompilerParams(
            collective_id=0, has_side_effects=True, vmem_limit_bytes=60 * 2**20
        ),
        cost_estimate=pl.CostEstimate(
            flops=2 * cols * tokens * width * wide + 6 * n * count * width * units,
            bytes_accessed=16 * 2**20,
            transcendentals=QUERY_HEADS * tokens * n * tokens,
        ),
    )(query, key, value, ids, gates, gain, hidden, weight, gate, up, down)


def per_device(
    hidden_in,
    queries,
    keys,
    values,
    out_weight,
    norm_gain,
    w_gate,
    w_up,
    w_down_t,
    expert_ids,
    route_gates,
):
    tokens_here = hidden_in.shape[2]
    moved = run_layer(
        queries[0, 0],
        keys[0, 0],
        values[0, 0],
        expert_ids[0, 0].reshape(1, tokens_here),
        route_gates[0, 0].reshape(1, tokens_here),
        norm_gain,
        hidden_in[0, 0],
        out_weight[0],
        w_gate[0, 0].T,
        w_up[0, 0].T,
        w_down_t[0, 0].T,
    )
    return moved.reshape(1, 1, tokens_here, D)


def solution(mesh):
    return jax.shard_map(
        per_device,
        mesh=mesh,
        in_specs=(
            P("section", "exp", "ctx", None),
            P("section", "exp", "ctx", None),
            P("section", "exp", "ctx", None),
            P("section", "exp", "ctx", None),
            P("section", "ctx", None),
            P("section", None),
            P("section", "exp", None, "ctx"),
            P("section", "exp", None, "ctx"),
            P("section", "exp", None, "ctx"),
            P("section", "exp", "ctx", None),
            P("section", "exp", "ctx", None),
        ),
        out_specs=P("section", "exp", "ctx", None),
        check_vma=False,
    )
```

time: 364 us -> 303 us (0.83)
  waiting for transfers between devices: 39.2 us -> 0 us
  Pallas kernels: 276 us -> 301 us
  blocking collectives: 16.6 us -> 0 us
  starting transfers between devices: 15.3 us -> 0 us
  local copies, waits for them, and re-layouts: 10.4 us -> 2.29 us
    pallas_call x2 -> x1, Pallas kernels: 276 us -> 301 us  [run_layer(): pl.pallas_call(functools.partial(layer_kernel, n, cols, sections, capacit...]
    ppermute x1 -> x0, waiting for transfers between devices: 22.1 us -> none  [passed_along(): lax.ppermute(array, axis, [(i, (i + by) % count) for i in range(count)])]
    all_to_all x1 -> x0, waiting for transfers between devices: 17 us -> none  [per_device(): lax.all_to_all(leaving, 'exp', split_axis=0, concat_axis=0, tiled=True)]
    all_to_all x1 -> x0, blocking collectives: 16.6 us -> none  [per_device(): lax.all_to_all(layer_out, 'exp', split_axis=0, concat_axis=0, tiled=True,...]
    all_to_all x1 -> x0, starting transfers between devices: 13.3 us -> none  [per_device(): lax.all_to_all(leaving, 'exp', split_axis=0, concat_axis=0, tiled=True)]
  transfers between devices with their start and end apart: 2 -> 0, of which waited for: 2 -> 0; matrix products, arithmetic and copies ran while one was open for 0% -> 0% of each run, Pallas kernels for 0% -> 0%
where the time goes in v4:
time: 303 us
  Pallas kernels  301 us (99%)
    pallas_call x1, Pallas kernels, run_layer(): pl.pallas_call(functools.partial(layer_kernel, n, cols, sections, capacit...  301 us

profile of v4, /device:TPU:1, one launch (start us, length us, event | category | flops | bytes accessed | tf_op | source)
XLA Modules:
  0.0 303.2 jit_solution(17357298267000533710)
XLA Ops:
  0.0 300.9 %shard_map.109 = bf16[128,4096]{1,0:T(8,128)(2,1)} custom-call(bf16[128,4096]{1,0:T(8,128)(2,1)} %bitcast.22, bf16[128,256]{1,0:T(8,128)(2,1)} %bitcast.24, bf16[128,256]{1,0:T(8,128)(2,1)} %bitcast.25, s32[1,128]{1,0:T(1,128)} %bitcast.26, f32[1,128]{1,0:T(1,128)} %bitcast.27, bf16[1,4096]{1,0:T(2,128)(2,1)} %gain.1, bf16[128,4096]{1,0:T(8,128)(2,1)} %bitcast.23, ...), custom_call_target="tpu_custom_call" | custom-call | flops 10334765056 | bytes 16777216 | tf_op jit(solution)/shard_map/pallas_call | solution.py:672
  300.9 2.3 copy.13

commit v5 on v4

--- a/solution.py
+++ b/solution.py
@@ -48,18 +48,22 @@
     cols,
     sections,
     capacity,
-    query,
-    key_in,
-    value_in,
-    ids_in,
-    gates_in,
-    gain,
+    query_any,
+    key_any,
+    value_any,
+    ids_any,
+    gates_any,
+    gain_any,
     hidden_any,
     weight_any,
     gate_any,
     up_any,
     down_any,
     result,
+    query,
+    ids_in,
+    gates_in,
+    gain,
     kv,
     mixed,
     weight,
@@ -156,6 +160,15 @@
         ),
         pltpu.make_async_copy(hidden_any.at[:, lanes(x * wide, wide)], hidden.at[x], local_sem.at[2]),
         pltpu.make_async_copy(down_any.at[:, lanes(z * part, part)], down.at[0], local_sem.at[3]),
+        pltpu.make_async_copy(query_any, query, local_sem.at[4]),
+        pltpu.make_async_copy(gain_any, gain, local_sem.at[5]),
+    ]
+    kv_width = key_any.shape[1]
+    first_loads = [
+        pltpu.make_async_copy(key_any, kv.at[z, :, pl.ds(0, kv_width)], local_sem.at[6]),
+        pltpu.make_async_copy(value_any, kv.at[z, :, pl.ds(kv_width, kv_width)], local_sem.at[7]),
+        pltpu.make_async_copy(ids_any, ids_in, local_sem.at[8]),
+        pltpu.make_async_copy(gates_any, gates_in, local_sem.at[9]),
     ]
     expert_loads = [
         pltpu.make_async_copy(
@@ -167,10 +180,10 @@
         for h in range(streams)
         for q in range(cols)
     ]
-    for copy in loads + expert_loads:
+    for copy in first_loads + loads + expert_loads:
         copy.start()
-    kv[z, :, 0 : key_in.shape[1]] = key_in[...]
-    kv[z, :, key_in.shape[1] :] = value_in[...]
+    for copy in first_loads:
+        copy.wait()
     ids[x] = jnp.broadcast_to(ids_in[...], ids.shape[1:])
     gates[x] = jnp.transpose(jnp.broadcast_to(gates_in[...], (128, tokens)))
     greet(
@@ -179,49 +192,53 @@
         + [{"section": at, "exp": q * CORES + core} for at in (after, before) for q in range(cols)]
     )
 
-    def kv_step(s):
+    def ring_pieces(s, h, place_up, place_down, sems):
+        up_send, up_recv, down_send, down_recv = sems
+        copies = []
+        if s < half or h % 2 == 0:
+            src, dst = place_up
+            copies.append(to_peer(up_z, src, dst, up_send.at[s - 1, h], up_recv.at[s - 1, h]))
+        if s < half or h % 2 == 1:
+            src, dst = place_down
+            copies.append(to_peer(down_z, src, dst, down_send.at[s - 1, h], down_recv.at[s - 1, h]))
+        return copies
+
+    kv_pieces, weight_pieces = kr_send.shape[1], wr_send.shape[1]
+
+    def kv_step(s, h):
         a, b = lax.rem(z + n + 1 - s, n), lax.rem(z + s - 1, n)
-        cut = tokens // 2
-        one, two = kv.at[a], kv.at[b]
-        if s == half:
-            one, two = kv.at[a, pl.ds(0, cut)], kv.at[b, pl.ds(cut, cut)]
-        return (
-            to_peer(up_z, one, one, kr_send.at[s - 1], kr_recv.at[s - 1]),
-            to_peer(down_z, two, two, kl_send.at[s - 1], kl_recv.at[s - 1]),
-        )
-
-    def weight_step(s):
+        size = tokens // kv_pieces
+        one, two = kv.at[a, pl.ds(h * size, size)], kv.at[b, pl.ds(h * size, size)]
+        return ring_pieces(s, h, (one, one), (two, two), (kr_send, kr_recv, kl_send, kl_recv))
+
+    def weight_step(s, h):
         a, b = lax.rem(z + n + 1 - s, n), lax.rem(z + s - 1, n)
-        cut = chunk // 2
-        one, two = weight.at[a, core], weight.at[b, core]
-        if s == half:
-            one, two = weight.at[a, core, pl.ds(0, cut)], weight.at[b, core, pl.ds(cut, cut)]
-        own = weight_any.at[:, lanes(x * wide + core * chunk, chunk)]
-        return (
-            to_peer(up_z, own if s == 1 else one, one, wr_send.at[s - 1], wr_recv.at[s - 1]),
-            to_peer(down_z, own if s == 1 else two, two, wl_send.at[s - 1], wl_recv.at[s - 1]),
-        )
-
-    def share(off):
+        size = chunk // weight_pieces
+        window = pl.ds(h * size, size)
+        one, two = weight.at[a, core, window], weight.at[b, core, window]
+        own = weight_any.at[window, lanes(x * wide + core * chunk, chunk)]
+        return ring_pieces(
+            s,
+            h,
+            (own if s == 1 else one, one),
+            (own if s == 1 else two, two),
+            (wr_send, wr_recv, wl_send, wl_recv),
+        )
+
+    def share(off, h, side):
         k = lax.rem(z + off, n)
-        return to_peer(
-            sibling, weight.at[k, core], weight.at[k, core], sib_send.at[off], sib_recv.at[off]
-        )
-
-    def shared(off):
-        k = lax.rem(z + off, n)
-        return to_peer(
-            sibling, weight.at[k, 1 - core], weight.at[k, 1 - core], sib_send.at[off], sib_recv.at[off]
-        )
-
-    def weight_arrived(s):
-        for copy in weight_step(s):
+        size = chunk // weight_pieces
+        block = weight.at[k, side, pl.ds(h * size, size)]
+        return to_peer(sibling, block, block, sib_send.at[off, h], sib_recv.at[off, h])
+
+    def weight_arrived(s, h):
+        for copy in weight_step(s, h):
             copy.wait_recv()
         if s < half:
-            for copy in weight_step(s + 1):
+            for copy in weight_step(s + 1, h):
                 copy.start()
-            share(n - s).start()
-        share(s).start()
+            share(n - s, h, core).start()
+        share(s, h, core).start()
 
     small = []
     for d in range(1, cols):
@@ -235,9 +252,9 @@
             small.append(
                 to_peer(same[d], src, dst, small_send.at[d, at], small_recv.at[cols - d, at])
             )
-    now = kv_step(1)
-    for copy in now:
-        copy.start()
+    for h in range(kv_pieces):
+        for copy in kv_step(1, h):
+            copy.start()
     for copy in small:
         copy.start()
 
@@ -246,15 +263,19 @@
     bias[...] = jnp.where(row >= column, 0.0, -1e30)
     residual[...] = jnp.zeros_like(residual)
 
+    acc[...] = jnp.zeros_like(acc)
     for s in range(1, half + 1):
-        for copy in now:
-            copy.wait_recv()
-        if s < half:
-            now = kv_step(s + 1)
-            for copy in now:
-                copy.start()
-    for copy in weight_step(1):
-        copy.start()
+        for h in range(kv_pieces):
+            for copy in kv_step(s, h):
+                copy.wait_recv()
+            if s < half:
+                for copy in kv_step(s + 1, h):
+                    copy.start()
+        for at, h in ((1,0),(2,1),(3,2),(3,3)):
+            if s == at:
+                for copy in weight_step(1, h):
+                    copy.start()
+    loads[4].wait()
 
     def place(j):
         odd = lax.rem(j, 2)
@@ -291,7 +312,8 @@
 
         @pl.when(off > 0)
         def _():
-            shared(off).wait_recv()
+            for h in range(weight_pieces):
+                share(off, h, 1 - core).wait_recv()
 
         left = mixed[k].reshape(cols * tokens, chunk)
         for side in range(CORES):
@@ -323,25 +345,26 @@
         def _():
             chunk_forward(j - 1)
 
-        @pl.when(j == 2)
+        @pl.when(j == 1)
         def _():
             loads[0].wait()
             loads[1].wait()
-            weight_arrived(1)
-
-        @pl.when(j == 5)
-        def _():
-            weight_arrived(2)
+
+        for at, (s, h) in ((0, (1, 0)), (1, (1, 1)), (1, (1, 2)), (2, (1, 3)), (3, (2, 0)), (3, (2, 1)), (4, (2, 2)), (5, (2, 3)), (6, (3, 0)), (6, (3, 1)), (7, (3, 2)), (7, (3, 3))):
+
+            @pl.when(j == at)
+            def _():
+                weight_arrived(s, h)
 
         @pl.when(j >= 3)
         def _():
             project(j - 3)
 
     chunk_forward(n - 1)
-    weight_arrived(3)
     project(n - 3)
     project(n - 2)
-    weight_arrived(4)
+    for h in range(weight_pieces):
+        weight_arrived(half, h)
     downs = []
     for d in (4, 3, 5, 2, 6, 1, 7):
         peer = lax.rem(z + d, n)
@@ -358,6 +381,7 @@
     for copy in small:
         copy.wait_recv()
     loads[2].wait()
+    loads[5].wait()
 
     expert = lax.broadcasted_iota(I32, (experts, tokens), 0)
     earlier = lax.broadcasted_iota(I32, (tokens, tokens), 0) < lax.broadcasted_iota(
@@ -439,6 +463,52 @@
             copies.append(to_peer(down_z, src, dst, rl_send.at[s - 1, h], rl_recv.at[s - 1, h]))
         return copies
 
+    order = [0, 1, 7, 2, 6, 3, 5, 4]
+    ready = [order.index(r) for r in range(n)]
+    bounds = ((0, 3), (3, 7), (7, 8))
+
+    def hid_step(part_at, s):
+        first, end = bounds[part_at]
+        blocks = pl.ds(first, end - first)
+        one, here = hid.at[(n + 1 - s) % n, blocks], hid.at[n - s, blocks]
+        two, there = hid.at[s - 1, blocks], hid.at[s, blocks]
+        if s == half:
+            cut = 128
+            one, here = one.at[:, pl.ds(0, cut)], here.at[:, pl.ds(0, cut)]
+            two, there = two.at[:, pl.ds(cut, count + pair - cut)], there.at[:, pl.ds(cut, count + pair - cut)]
+        return (
+            to_peer(up_z, one, here, hr_send.at[part_at, s - 1], hr_recv.at[part_at, s - 1]),
+            to_peer(down_z, two, there, hl_send.at[part_at, s - 1], hl_recv.at[part_at, s - 1]),
+        )
+
+    def hid_start(part_at, s):
+        copies = hid_step(part_at, s)
+        for copy in copies:
+            copy.start()
+        sent.extend(copies)
+        hid_now[part_at] = copies
+
+    def hid_arrived(part_at, s):
+        for copy in hid_now[part_at]:
+            copy.wait_recv()
+        if s < half:
+            hid_start(part_at, s + 1)
+
+    def unpack(r, p):
+        packed = hid[r, p]
+        end = packed[count : count + pair]
+        rest = jnp.concatenate([end[:, 0 : units - 128], end[:, units - 128 :]], axis=0)
+        return jnp.concatenate([packed[0:count], rest], axis=1)
+
+    def shrink(part_at, *shards):
+        @pl.loop(*bounds[part_at])
+        def _(p):
+            off, _ = place(p)
+            for r in shards:
+                acc[lax.rem(z + r + off, n)] += jnp.dot(
+                    unpack(r, p), down[r], preferred_element_type=F32
+                )
+
     def expand(r):
         gate_part, up_part = 0.0, 0.0
         for h in range(streams):
@@ -446,9 +516,8 @@
             gate_part += across(block, gate[h])
             up_part += across(block, up[h])
         shown = (gate_part / (1.0 + jnp.exp(-gate_part)) * up_part).astype(BF16)
-        owner = lax.rem(z + r, n)
-        hid[0, owner, 0:count, :] = shown[:, 0:128]
-        hid[0, owner, count : count + pair, :] = jnp.concatenate(
+        hid[0, ready[r], 0:count, :] = shown[:, 0:128]
+        hid[0, ready[r], count : count + pair, :] = jnp.concatenate(
             [shown[0:pair, 128:units], shown[pair:count, 128:units]], axis=1
         )
 
@@ -464,9 +533,11 @@
         steps[1, h] = rows_step(1, h)
         for copy in steps[1, h]:
             copy.start()
+        sent += steps[1, h]
     for copy in expert_loads:
         copy.wait()
     expand(0)
+    hid_now = {}
     for s in range(1, half + 1):
         for h in range(streams):
             for copy in steps[s, h]:
@@ -475,58 +546,42 @@
                 steps[s + 1, h] = rows_step(s + 1, h)
                 for copy in steps[s + 1, h]:
                     copy.start()
-        expand(s)
+                sent += steps[s + 1, h]
+        if s > 1:
+            hid_arrived(0, s - 1)
         if s < half:
+            expand(s)
             expand(n - s)
-    for copies in steps.values():
-        sent += copies
-
-    def hid_step(s):
-        one, two = hid.at[(n + 1 - s) % n], hid.at[s - 1]
-        here, there = hid.at[n - s], hid.at[s]
-        if s == half:
-            one, here = one.at[pl.ds(0, half)], here.at[pl.ds(0, half)]
-            two, there = two.at[pl.ds(half, half)], there.at[pl.ds(half, half)]
-        return (
-            to_peer(up_z, one, here, hr_send.at[s - 1], hr_recv.at[s - 1]),
-            to_peer(down_z, two, there, hl_send.at[s - 1], hl_recv.at[s - 1]),
-        )
-
-    def unpack(r, b):
-        packed = hid[r, b]
-        end = packed[count : count + pair]
-        rest = jnp.concatenate([end[:, 0 : units - 128], end[:, units - 128 :]], axis=0)
-        return jnp.concatenate([packed[0:count], rest], axis=1)
-
-    def shrink(r, b):
-        return jnp.dot(unpack(r, b), down[r], preferred_element_type=F32)
-
-    now = hid_step(1)
-    sent += now
-    for copy in now:
-        copy.start()
-    loads[3].wait()
-    for copy in downs:
-        copy.wait_recv()
-
-    @pl.loop(0, n)
-    def _(b):
-        acc[b] = shrink(0, b)
-
-    for s in range(1, half):
-        for copy in now:
-            copy.wait_recv()
-        now = hid_step(s + 1)
-        sent += now
-        for copy in now:
-            copy.start()
-
-        @pl.loop(0, n)
-        def _(b):
-            acc[b] += shrink(s, b) + shrink(n - s, b)
-
-    for copy in now:
-        copy.wait_recv()
+        else:
+            expand(half)
+        if s == 1:
+            hid_start(0, 1)
+            loads[3].wait()
+            for copy in downs:
+                copy.wait_recv()
+            shrink(0, 0)
+        elif s == 2:
+            shrink(0, 1, n - 1)
+        elif s == 3:
+            hid_start(1, 1)
+            shrink(0, 2, n - 2)
+            shrink(1, 0)
+    hid_start(2, 1)
+    hid_arrived(1, 1)
+    shrink(0, 3, n - 3)
+    shrink(1, 1, n - 1)
+    hid_arrived(2, 1)
+    shrink(2, 0, 1, n - 1)
+    hid_arrived(1, 2)
+    hid_arrived(2, 2)
+    shrink(1, 2, n - 2)
+    shrink(2, 2, n - 2)
+    hid_arrived(1, 3)
+    hid_arrived(2, 3)
+    shrink(1, 3, n - 3)
+    shrink(2, 3, n - 3)
+    for part_at in range(len(bounds)):
+        hid_arrived(part_at, half)
 
     def leave(d, i):
         b = lax.rem(z + d, n)
@@ -544,7 +599,7 @@
         for d in (4, 3, 5, 2, 6, 1, 7, 0):
             b = lax.rem(z + d, n)
             block = acc[b, :, window] + jnp.dot(
-                unpack(half, b), down[half, :, window], preferred_element_type=F32
+                unpack(half, ready[(d + half) % n]), down[half, :, window], preferred_element_type=F32
             )
             if d == 0:
                 out[z, :, window] = block.astype(BF16)
@@ -641,10 +696,15 @@
     for copy in small + sums + sent + downs:
         copy.wait_send()
     for s in range(1, half + 1):
-        for copy in kv_step(s) + weight_step(s):
-            copy.wait_send()
+        for h in range(kv_pieces):
+            for copy in kv_step(s, h):
+                copy.wait_send()
+        for h in range(weight_pieces):
+            for copy in weight_step(s, h):
+                copy.wait_send()
     for off in range(1, n):
-        share(off).wait_send()
+        for h in range(weight_pieces):
+            share(off, h, core).wait_send()
 
     @pl.loop(0, n)
     def _(j):
@@ -667,14 +727,16 @@
     pieces = part // 128
     dma = pltpu.SemaphoreType.DMA
     anywhere = pl.BlockSpec(memory_space=pl.ANY)
-    in_vmem = pl.BlockSpec(memory_space=pltpu.VMEM)
-    ring = [dma((n // 2,))] * 4
     return pl.pallas_call(
         functools.partial(layer_kernel, n, cols, sections, capacity),
         out_shape=jax.ShapeDtypeStruct((tokens, width), BF16),
-        in_specs=[in_vmem] * 6 + [anywhere] * 5,
-        out_specs=in_vmem,
+        in_specs=[anywhere] * 11,
+        out_specs=anywhere,
         scratch_shapes=[
+            pltpu.VMEM((tokens, width), BF16),
+            pltpu.VMEM(ids.shape, I32),
+            pltpu.VMEM(gates.shape, F32),
+            pltpu.VMEM(gain.shape, BF16),
             pltpu.VMEM((n, tokens, 2 * key.shape[1]), BF16),
             pltpu.VMEM((n, cols, tokens, part), BF16),
             pltpu.VMEM((n, CORES, part, part), BF16),
@@ -697,20 +759,20 @@
             pltpu.VMEM((n, count, part), BF16),
             pltpu.VMEM((experts, count // CORES, wide), BF16),
             pltpu.VMEM((pieces, wide // part, cols, tokens, 128), BF16),
-            dma((4,)),
+            dma((10,)),
             dma((streams, cols)),
             dma((streams, cols)),
         ]
-        + ring
-        + ring
-        + [dma((n,))] * 2
+        + [dma((n // 2, 2))] * 4
+        + [dma((n // 2, 4))] * 4
+        + [dma((n, 4))] * 2
         + [dma((n, 4))] * 2
         + [dma((cols, 3))] * 2
         + [dma((cols,))] * 2
         + [dma((n,))] * 2
         + [dma((experts, streams))] * 2
         + [dma((n // 2, streams))] * 4
-        + ring
+        + [dma((3, n // 2))] * 4
         + [dma((n, pieces))] * 2
         + [dma((n, CORES, pieces)), dma((experts, wide // part, pieces))]
         + [dma((pieces, wide // part, cols))] * 2,

time: 303 us -> 292 us (0.964)
  Pallas kernels: 301 us -> 289 us
    pallas_call x1, Pallas kernels: 301 us -> 289 us  [run_layer(): pl.pallas_call(functools.partial(layer_kernel, n, cols, sections, capacit...]
where the time goes in v5:
time: 292 us; the launch traced here: 291 us
  Pallas kernels  289 us (99%)
    pallas_call x1, Pallas kernels, run_layer(): pl.pallas_call(functools.partial(layer_kernel, n, cols, sections, capacit...  289 us

profile of v5, /device:TPU:1, one launch (start us, length us, event | category | flops | bytes accessed | tf_op | source)
XLA Modules:
  0.0 291.4 jit_solution(907204135368840611)
XLA Ops:
  0.0 289.1 %shard_map.109 = bf16[128,4096]{1,0:T(8,128)(2,1)} custom-call(bf16[128,4096]{1,0:T(8,128)(2,1)} %bitcast.22, bf16[128,256]{1,0:T(8,128)(2,1)} %bitcast.24, bf16[128,256]{1,0:T(8,128)(2,1)} %bitcast.25, s32[1,128]{1,0:T(1,128)} %bitcast.26, f32[1,128]{1,0:T(1,128)} %bitcast.27, bf16[1,4096]{1,0:T(2,128)(2,1)} %gain_any.1, bf16[128,4096]{1,0:T(8,128)(2,1)} %bitcast.23, ...), custom_call_target="tpu_custom_call" | custom-call | flops 10334765056 | bytes 16777216 | tf_op jit(solution)/shard_map/pallas_call | solution.py:730
  289.1 2.3 copy.13

commit v6 on v5

--- a/solution.py
+++ b/solution.py
@@ -29,10 +29,14 @@
 
 
 def greet(peers):
-    barrier = pltpu.get_barrier_semaphore()
     for peer in peers:
-        pl.semaphore_signal(barrier, inc=1, device_id=peer, device_id_type=MESH)
-    pl.semaphore_wait(barrier, len(peers))
+        pl.semaphore_signal(
+            pltpu.get_barrier_semaphore(), inc=1, device_id=peer, device_id_type=MESH
+        )
+
+
+def greeted(peers):
+    pl.semaphore_wait(pltpu.get_barrier_semaphore(), len(peers))
 
 
 def lanes(start, size):
@@ -151,6 +155,13 @@
     sibling = {"exp": x * CORES + 1 - core}
     after, before = lax.rem(section + 1, sections), lax.rem(section + sections - 1, sections)
 
+    peers = (
+        [{"ctx": lax.rem(z + d, n)} for d in range(1, n)]
+        + [{"exp": lax.rem(me + d, experts)} for d in range(1, experts)]
+        + [{"section": at, "exp": q * CORES + core} for at in (after, before) for q in range(cols)]
+    )
+    greet(peers)
+
     loads = [
         pltpu.make_async_copy(
             weight_any.at[:, lanes(x * wide, chunk)], weight.at[z, 0], local_sem.at[0]
@@ -180,17 +191,13 @@
         for h in range(streams)
         for q in range(cols)
     ]
-    for copy in first_loads + loads + expert_loads:
+    for copy in first_loads + loads:
         copy.start()
     for copy in first_loads:
         copy.wait()
     ids[x] = jnp.broadcast_to(ids_in[...], ids.shape[1:])
     gates[x] = jnp.transpose(jnp.broadcast_to(gates_in[...], (128, tokens)))
-    greet(
-        [{"ctx": lax.rem(z + d, n)} for d in range(1, n)]
-        + [{"exp": lax.rem(me + d, experts)} for d in range(1, experts)]
-        + [{"section": at, "exp": q * CORES + core} for at in (after, before) for q in range(cols)]
-    )
+    greeted(peers)
 
     def ring_pieces(s, h, place_up, place_down, sems):
         up_send, up_recv, down_send, down_recv = sems
@@ -255,7 +262,7 @@
     for h in range(kv_pieces):
         for copy in kv_step(1, h):
             copy.start()
-    for copy in small:
+    for copy in small + expert_loads:
         copy.start()
 
     row = lax.broadcasted_iota(I32, (tokens, n * tokens), 0) + z * tokens

time: 292 us -> 290 us (level)
  no operation moved by 1% of the time
where the time goes in v6:
time: 290 us
  Pallas kernels  287 us (99%)
    pallas_call x1, Pallas kernels, run_layer(): pl.pallas_call(functools.partial(layer_kernel, n, cols, sections, capacit...  287 us

profile of v6, /device:TPU:1, one launch (start us, length us, event | category | flops | bytes accessed | tf_op | source)
XLA Modules:
  0.0 289.8 jit_solution(1091120208976199559)
XLA Ops:
  0.0 287.5 %shard_map.109 = bf16[128,4096]{1,0:T(8,128)(2,1)} custom-call(bf16[128,4096]{1,0:T(8,128)(2,1)} %bitcast.22, bf16[128,256]{1,0:T(8,128)(2,1)} %bitcast.24, bf16[128,256]{1,0:T(8,128)(2,1)} %bitcast.25, s32[1,128]{1,0:T(1,128)} %bitcast.26, f32[1,128]{1,0:T(1,128)} %bitcast.27, bf16[1,4096]{1,0:T(2,128)(2,1)} %gain_any.1, bf16[128,4096]{1,0:T(8,128)(2,1)} %bitcast.23, ...), custom_call_target="tpu_custom_call" | custom-call | flops 10334765056 | bytes 16777216 | tf_op jit(solution)/shard_map/pallas_call | solution.py:737
  287.5 2.3 copy.13

commit v7 on v6

--- a/solution.py
+++ b/solution.py
@@ -268,7 +268,6 @@
     row = lax.broadcasted_iota(I32, (tokens, n * tokens), 0) + z * tokens
     column = lax.broadcasted_iota(I32, (tokens, n * tokens), 1)
     bias[...] = jnp.where(row >= column, 0.0, -1e30)
-    residual[...] = jnp.zeros_like(residual)
 
     acc[...] = jnp.zeros_like(acc)
     for s in range(1, half + 1):
@@ -327,6 +326,23 @@
             residual[:, side * chunk : (side + 1) * chunk] += jnp.dot(
                 left, weight[k, side], preferred_element_type=F32
             )
+
+    def places():
+        expert = lax.broadcasted_iota(I32, (experts, tokens), 0)
+        earlier = lax.broadcasted_iota(I32, (tokens, tokens), 0) < lax.broadcasted_iota(
+            I32, (tokens, tokens), 1
+        )
+        earlier = jnp.where(earlier, 1.0, 0.0).astype(BF16)
+        placed = []
+        for q in range(cols):
+            chosen = ids[q]
+            named = jnp.where(expert == chosen, 1.0, 0.0)
+            ahead = jnp.dot(named.astype(BF16), earlier, preferred_element_type=F32)
+            rank = jnp.sum(ahead * named, axis=0, keepdims=True)
+            placed.append(
+                (chosen[0:1] * (cols * capacity) + q * capacity).astype(F32) + rank
+            )
+        return jnp.concatenate(placed, axis=1)
 
     scale = math.log2(math.e) / math.sqrt(HEAD_SIZE)
 
@@ -348,6 +364,19 @@
         for copy in chunk_first(j):
             copy.start()
 
+        @pl.when(j == 1)
+        def _():
+            for copy in small:
+                copy.wait_recv()
+            loads[2].wait()
+            loads[5].wait()
+            residual[...] = hidden[...].reshape(cols * tokens, wide).astype(F32)
+
+        @pl.when(j == 2)
+        def _():
+            slot = lax.broadcasted_iota(I32, selector.shape, 0).astype(F32)
+            selector[...] = jnp.where(slot == places(), 1.0, 0.0).astype(BF16)
+
         @pl.when(j >= 1)
         def _():
             chunk_forward(j - 1)
@@ -367,11 +396,6 @@
         def _():
             project(j - 3)
 
-    chunk_forward(n - 1)
-    project(n - 3)
-    project(n - 2)
-    for h in range(weight_pieces):
-        weight_arrived(half, h)
     downs = []
     for d in (4, 3, 5, 2, 6, 1, 7):
         peer = lax.rem(z + d, n)
@@ -385,38 +409,19 @@
             )
         )
         downs[-1].start()
-    for copy in small:
-        copy.wait_recv()
-    loads[2].wait()
-    loads[5].wait()
-
-    expert = lax.broadcasted_iota(I32, (experts, tokens), 0)
-    earlier = lax.broadcasted_iota(I32, (tokens, tokens), 0) < lax.broadcasted_iota(
-        I32, (tokens, tokens), 1
-    )
-    earlier = jnp.where(earlier, 1.0, 0.0).astype(BF16)
-    placed = []
-    for q in range(cols):
-        chosen = ids[q]
-        named = jnp.where(expert == chosen, 1.0, 0.0)
-        ahead = jnp.dot(named.astype(BF16), earlier, preferred_element_type=F32)
-        rank = jnp.sum(ahead * named, axis=0, keepdims=True)
-        placed.append(
-            (chosen[0:1] * (cols * capacity) + q * capacity).astype(F32) + rank
-        )
-    placed = jnp.concatenate(placed, axis=1)
-    slot = lax.broadcasted_iota(I32, selector.shape, 0).astype(F32)
-    selector[...] = jnp.where(slot == placed, 1.0, 0.0).astype(BF16)
-    placed_t = jnp.transpose(jnp.broadcast_to(placed, (8, cols * tokens)))[:, 0:1]
-    slot = lax.broadcasted_iota(I32, selector_t.shape, 1).astype(F32)
-    selector_t[...] = jnp.where(slot == placed_t, 1.0, 0.0).astype(BF16)
-
+    chunk_forward(n - 1)
+    project(n - 3)
+    project(n - 2)
+    for h in range(weight_pieces):
+        weight_arrived(half, h)
     project(n - 1)
-    residual[...] += hidden[...].reshape(cols * tokens, wide).astype(F32)
     res = residual[...]
+    squared = res[:, 0:128] * res[:, 0:128]
+    for at in range(128, wide, 128):
+        squared += res[:, at : at + 128] * res[:, at : at + 128]
     squares[x] = lax.dot_general(
-        jnp.ones((8, wide), F32),
-        res * res,
+        jnp.ones((8, 128), F32),
+        squared,
         (((1,), (1,)), ((), ())),
         precision=lax.Precision.HIGHEST,
         preferred_element_type=F32,
@@ -544,6 +549,9 @@
     for copy in expert_loads:
         copy.wait()
     expand(0)
+    placed_t = jnp.transpose(jnp.broadcast_to(places(), (8, cols * tokens)))[:, 0:1]
+    slot = lax.broadcasted_iota(I32, selector_t.shape, 1).astype(F32)
+    selector_t[...] = jnp.where(slot == placed_t, 1.0, 0.0).astype(BF16)
     hid_now = {}
     for s in range(1, half + 1):
         for h in range(streams):

time: 290 us -> 289 us (level)
  no operation moved by 1% of the time
where the time goes in v7:
time: 289 us
  Pallas kernels  287 us (99%)
    pallas_call x1, Pallas kernels, run_layer(): pl.pallas_call(functools.partial(layer_kernel, n, cols, sections, capacit...  287 us

profile of v7, /device:TPU:1, one launch (start us, length us, event | category | flops | bytes accessed | tf_op | source)
XLA Modules:
  0.0 288.9 jit_solution(7872787322172559380)
XLA Ops:
  0.0 286.6 %shard_map.109 = bf16[128,4096]{1,0:T(8,128)(2,1)} custom-call(bf16[128,4096]{1,0:T(8,128)(2,1)} %bitcast.22, bf16[128,256]{1,0:T(8,128)(2,1)} %bitcast.24, bf16[128,256]{1,0:T(8,128)(2,1)} %bitcast.25, s32[1,128]{1,0:T(1,128)} %bitcast.26, f32[1,128]{1,0:T(1,128)} %bitcast.27, bf16[1,4096]{1,0:T(2,128)(2,1)} %gain_any.1, bf16[128,4096]{1,0:T(8,128)(2,1)} %bitcast.23, ...), custom_call_target="tpu_custom_call" | custom-call | flops 10334765056 | bytes 16777216 | tf_op jit(solution)/shard_map/pallas_call | solution.py:745
  286.6 2.3 copy.13
